TPU v7x, 32 devices: a whole 2x2x4 slice. The times are simulated.
32 devices in a mesh: dp: 16 (over z, y, core), fsdp: 2 (over x).
Axes of the slice: x: 2, y: 2, z: 4, core: 2. Of those that a mesh axis runs over, the one named last changes fastest.
Arguments:
- context: bfloat16 [8192, 2048], P(('dp', 'fsdp')), may hold values from -6 to 6
- residual: bfloat16 [8192, 2048], P(('dp', 'fsdp')), may hold values from -6 to 6
- weight: bfloat16 [2048, 2048], P('fsdp'), may hold values from -0.125 to 0.125
- gain: bfloat16 [2048], replicated, may hold values from 0.099609375 to 1.8984375
- pattern: int32 [32, 16], P(('dp', 'fsdp')), may hold values from 0 to 1, as said below
- positive: int32 [64], P(('dp', 'fsdp')), may hold values from 0 to 1
Outputs:
- losses: float32 [64], P(('dp', 'fsdp'))
- grad_weight: float32 [2048, 2048], P('fsdp', 'dp')
Inputs may be any that keep to these rules, and one draw needn't show every extreme that they name: pattern is 0 or 1; row b always holds 1 at column b // 2 (its own block); rows hold different numbers of ones.
All inputs are finite; a program needn't handle non-finite values.
Results may differ from a plain program's by a relative error of at most 0.0046.
Values may be sent and summed in bfloat16 or wider, within the bound.
A program may use at most 64 MiB of HBM per device.

v0:
```python
import jax
import jax.numpy as jnp
from jax import lax
from jax.sharding import PartitionSpec as P


def body(context, residual, weight, gain, pattern, positive):
    rows = context.shape[0]
    seqs = positive.shape[0]
    length = rows // (2 * seqs)
    width = residual.shape[1]
    columns = context
    projected = jnp.dot(
        columns,
        lax.all_gather(weight, "fsdp", axis=0, tiled=True),
        preferred_element_type=jnp.float32,
    )
    hidden = residual.astype(jnp.float32) + projected
    inv = lax.rsqrt(jnp.mean(hidden * hidden, axis=1, keepdims=True) + 1e-05)
    gain_wide = gain.astype(jnp.float32)
    normed = hidden * inv * gain_wide
    pooled = normed.reshape(2 * seqs, length, width).mean(axis=1)
    scale = lax.rsqrt(jnp.sum(pooled * pooled, axis=1, keepdims=True) + 1e-06)
    unit = pooled * scale
    embed = unit.astype(jnp.bfloat16)
    query = embed[:seqs]
    premise = embed[seqs:]
    pool = lax.all_gather(premise, "dp", axis=0, tiled=True)
    blocks = lax.axis_size("dp")
    scores = 20.0 * lax.dot_general(
        query, pool, (((1,), (1,)), ((), ())), preferred_element_type=jnp.float32
    )
    allowed = jnp.repeat(pattern[0], seqs).astype(jnp.float32)[None, :]
    target = lax.axis_index("dp") * seqs + positive
    onehot = (jnp.arange(blocks * seqs, dtype=jnp.int32)[None, :] == target[:, None]).astype(
        jnp.float32
    )
    weighted = allowed * jnp.exp(scores)
    total = jnp.sum(weighted, axis=1, keepdims=True)
    losses = jnp.log(total[:, 0]) - jnp.sum(onehot * scores, axis=1)
    coeff = (weighted / total - onehot).astype(jnp.bfloat16)
    d_query = 20.0 * jnp.dot(coeff, pool, preferred_element_type=jnp.float32)
    d_pool = 20.0 * lax.dot_general(
        coeff, query, (((0,), (0,)), ((), ())), preferred_element_type=jnp.float32
    )
    d_premise = lax.psum_scatter(d_pool, "dp", scatter_dimension=0, tiled=True)
    d_embed = jnp.concatenate([d_query, d_premise], axis=0)
    d_pooled = (d_embed - unit * jnp.sum(unit * d_embed, axis=1, keepdims=True)) * scale
    d_normed = jnp.broadcast_to(d_pooled[:, None, :] / length, (2 * seqs, length, width)).reshape(
        rows, width
    )
    gated = d_normed * gain_wide
    d_hidden = (
        inv * gated - hidden * inv * inv * inv * jnp.mean(hidden * gated, axis=1, keepdims=True)
    ).astype(jnp.bfloat16)
    columns = d_hidden
    partial_columns = lax.psum_scatter(
        lax.dot_general(
            columns, context, (((0,), (0,)), ((), ())), preferred_element_type=jnp.float32
        ),
        "dp",
        scatter_dimension=0,
        tiled=True,
    )
    grad_weight = lax.psum_scatter(partial_columns, "fsdp", scatter_dimension=1, tiled=True).T
    return (losses, grad_weight)


def solution(mesh):
    return jax.shard_map(
        body,
        mesh=mesh,
        in_specs=(
            P(("dp", "fsdp"), None),
            P(("dp", "fsdp"), None),
            P("fsdp", None),
            P(),
            P(("dp", "fsdp"), None),
            P(("dp", "fsdp")),
        ),
        out_specs=(P(("dp", "fsdp")), P("fsdp", "dp")),
        check_vma=False,
    )
```

profile of v0, /device:TPU:0, one launch (start us, length us, event | category | flops | bytes accessed | tf_op | source)
XLA Modules:
  0.0 450.7 jit_solution(2131350224633718041)
XLA Ops:
  7.3 0.7 all-gather.3.cloned.1.call-update
  8.0 0.1 broadcast_in_dim.4
  8.1 0.1 convert_element_type.34
  8.2 0.6 dynamic-slice
  9.5 106.8 %all-gather.3.cloned.1.call-done = bf16[2048,2048]{1,0:T(8,128)(2,1)} async-done(((bf16[1024,2048]{1,0:T(8,128)(2,1)}), bf16[2048,2048]{1,0:T(8,128)(2,1)}) %all-gather.3.cloned.1.call-update) | async-done | bytes 8388624 | tf_op jit(solution)/shard_map/all_gather | solution.py:15
  116.3 6.1 %multiply_reduce_fusion = (f32[256]{0:T(256)S(1)}, f32[256,2048]{1,0:T(8,128)S(1)}) fusion(bf16[256,2048]{1,0:T(8,128)(2,1)S(1)} %copy-done, bf16[2048,2048]{1,0:T(8,128)(2,1)} %all-gather.3.cloned.1.call-done, bf16[256,2048]{1,0:T(8,128)(2,1)} %param.7), kind=kOutput, calls=%fused_computation.10 | convolution fusion | flops 2149580544 | bytes 12583936 | tf_op jit(solution)/shard_map/dot_general | solution.py:13
  122.4 0.4 bitcast_reduce_fusion
  122.8 0.1 multiply_reduce_fusion.2
  123.0 0.1 multiply_convert_fusion
  123.1 21.7 %all-gather = bf16[16,2,2048]{2,1,0:T(2,128)(2,1)S(1)} all-gather(bf16[1,2,2048]{2,1,0:T(2,128)(2,1)S(1)} %slice_bitcast_fusion), channel_id=1, replica_groups=mesh['dp'=16,'fsdp'=2] {'dp'}, dimensions={0}, use_global_device_ids=true | all-gather | bytes 139264 | tf_op jit(solution)/shard_map/all_gather | solution.py:28
  144.8 0.3 fusion.8
  145.1 1.0 convolution_multiply_fusion
  146.2 0.2 convolution_multiply_fusion.1
  146.4 85.0 %all-reduce.3.cloned.1.call-done = f32[32,2048]{1,0:T(8,128)} async-done(((f32[32,2048]{1,0:T(8,128)}), f32[32,2048]{1,0:T(8,128)}) %all-reduce.3.cloned.1.call-update) | async-done | bytes 262160
  231.4 0.8 constant_dynamic-slice_fusion
  232.2 0.2 multiply_reduce_fusion.1
  232.4 0.1 multiply_multiply_fusion.1
  232.5 0.2 fusion.4
  232.8 0.6 fusion.3
  233.4 8.1 %fusion.11 = f32[2048,2048]{1,0:T(8,128)} fusion(bf16[256,2048]{1,0:T(8,128)(2,1)S(1)} %fusion.3, bf16[256,2048]{1,0:T(8,128)(2,1)S(1)} %copy-done), kind=kOutput, calls=%fused_computation.35 | convolution fusion | flops 2147483648 | bytes 18874368 | tf_op jit(solution)/shard_map/dot_general | solution.py:58
  241.5 179.2 %reduce-scatter.3.cloned.1.call-done = f32[128,2048]{1,0:T(8,128)} async-done(((f32[2048,2048]{1,0:T(8,128)}), f32[128,2048]{1,0:T(8,128)}) %reduce-scatter.3.cloned.1.call-update) | async-done | bytes 1048592 | tf_op jit(solution)/shard_map/reduce_scatter | solution.py:57
  420.7 0.5 log_subtract_fusion
  421.3 20.9 %reduce-scatter.5.cloned.1.call-done = f32[128,1024]{1,0:T(8,128)} async-done(((f32[128,2048]{1,0:T(8,128)}), f32[128,1024]{1,0:T(8,128)}) %reduce-scatter.5.cloned.1.call-update) | async-done | bytes 524304 | tf_op jit(solution)/shard_map/reduce_scatter | solution.py:65
  442.2 2.0 copy.10
  (25 shorter events, 0.3 us)
Async XLA Ops:
  7.2 109.2 %copy-start = (bf16[256,2048]{1,0:T(8,128)(2,1)S(1)}, bf16[256,2048]{1,0:T(8,128)(2,1)}, u32[]{:S(2)}) copy-start(bf16[256,2048]{1,0:T(8,128)(2,1)} %param.6) | copy-start | bytes 3145732
  7.2 1.1 copy-start.4
  7.2 0.8 copy-start.2
  7.2 1.0 copy-start.1
  7.2 2.3 copy-start.3
  7.2 109.1 %all-gather.3.cloned.1.call-start = ((), (), s32[]{:S(2)}) async-start(), calls=%async_computation.2 | async-start | bytes 12582912 | tf_op jit(solution)/shard_map/all_gather | solution.py:15
  8.0 223.4 %all-reduce.3.cloned.1.call-start = ((), (), s32[]{:S(2)}) async-start(), calls=%async_computation.5 | async-start | bytes 524288
  146.1 274.6 %reduce-scatter.3.cloned.1.call-start = ((), (), s32[]{:S(2)}) async-start(), calls=%async_computation.3 | async-start | bytes 17825792 | tf_op jit(solution)/shard_map/reduce_scatter | solution.py:57
  241.5 200.7 %reduce-scatter.5.cloned.1.call-start = ((), (), s32[]{:S(2)}) async-start(), calls=%async_computation.4 | async-start | bytes 1572864 | tf_op jit(solution)/shard_map/reduce_scatter | solution.py:65
Sparse Core Ops, SparseCore 0:
  9.6 106.6 all-gather.2
  146.2 85.1 all-reduce.2
  241.6 179.0 reduce-scatter.2
  422.8 19.2 reduce-scatter.4
where the time goes:
time: 451 us
  waiting for transfers between devices  393 us (87%)
  blocking collectives  21.7 us (5%)
  matrix products  15.7 us (3%)
  between operations  14.6 us (3%)
    reduce_scatter x1, waiting for transfers between devices, body(): lax.psum_scatter(lax.dot_general(columns, context, (((0,), (0,)), ((), ()...  179 us
    all_gather x1, waiting for transfers between devices, body(): lax.all_gather(weight, 'fsdp', axis=0, tiled=True)  107 us
    unnamed x5, waiting for transfers between devices  85.7 us
    all_gather x1, blocking collectives, body(): pool = lax.all_gather(premise, 'dp', axis=0, tiled=True)  21.7 us
    reduce_scatter x1, waiting for transfers between devices, body(): lax.psum_scatter(partial_columns, 'fsdp', scatter_dimension=1, tiled=True)  20.9 us
  transfers between devices with their start and end apart: 4, of which 4 were waited for; matrix products, arithmetic and copies ran while one was open for 0% of the time, Pallas kernels for 0%

commit v1 on v0

v1 whole, which is shorter than its diff:
```python
import functools

import jax
import jax.numpy as jnp
import numpy as np
from jax import lax
from jax.experimental import pallas as pl
from jax.experimental.pallas import tpu as pltpu
from jax.sharding import PartitionSpec as P

MESH = pl.DeviceIdType.MESH
F32 = jnp.float32
BF16 = jnp.bfloat16
HIGH = lax.Precision.HIGHEST
NT = (((1,), (1,)), ((), ()))


def flip(index, mask):
    out = index
    bit = 1
    while bit <= mask:
        if mask & bit:
            out = out + bit * (1 - 2 * lax.rem(lax.div(index, bit), 2))
        bit *= 2
    return out


def count_copies(nd, nf):
    nz = nd // 4
    return (nf - 1) * 16 + (nf - 1) + nf + (nd - 1) + (2 * nf - 1) * nz + nz + nz - 1


def kernel(
    nd,
    nf,
    seqs,
    context_hbm,
    residual_hbm,
    weight_hbm,
    gain_ref,
    pattern_ref,
    positive_ref,
    spread_ref,
    select_ref,
    same_ref,
    rows_ref,
    loss_ref,
    grad_ref,
    ctx,
    res,
    wg,
    hid,
    invs,
    ctx_t,
    ctx_all,
    msg,
    pool,
    dhs,
    dh_all,
    y_send,
    y_recv,
    kept,
    z_send,
    z_recv,
    local_sem,
    send_sem,
    recv_sem,
):
    d = lax.axis_index("dp")
    f = lax.axis_index("fsdp")
    tokens, width = ctx.shape
    nz = nd // 4
    bw = width // nd
    core = lax.rem(d, 2)
    y = lax.rem(lax.div(d, 2), 2)
    z = lax.div(d, 4)
    spot = lax.rem(d, 8)
    depth = wg.shape[1] * wg.shape[2] * wg.shape[3]
    length = tokens // (2 * seqs)
    other = lambda k: lax.rem(f + k, nf)
    source = lambda k: lax.rem(f + nf - k, nf)

    started = []

    def send(src, dst, dd, ff):
        slot = len(started)
        copy = pltpu.make_async_remote_copy(
            src_ref=src,
            dst_ref=dst,
            send_sem=send_sem.at[slot],
            recv_sem=recv_sem.at[slot],
            device_id=(dd, ff),
            device_id_type=MESH,
        )
        copy.start()
        started.append(copy)
        return copy

    own = pltpu.make_async_copy(weight_hbm, wg.at[f], local_sem.at[0])
    own.start()
    load_ctx = pltpu.make_async_copy(context_hbm, ctx, local_sem.at[1])
    load_ctx.start()
    load_res = pltpu.make_async_copy(residual_hbm, res, local_sem.at[2])
    load_res.start()

    barrier = pltpu.get_barrier_semaphore()
    partners = [(lax.rem(d + s, nd), f) for s in range(1, nd)]
    partners += [(d, other(k)) for k in range(1, nf)]
    partners += [(flip(d, 1), other(k)) for k in range(1, nf)]
    for partner in partners:
        pl.semaphore_signal(barrier, inc=1, device_id=partner, device_id_type=MESH)
    pl.semaphore_wait(barrier, len(partners))

    direct = {}
    for h in range(2):
        for k in range(1, nf):
            direct[h, k] = send(weight_hbm.at[spot, h], wg.at[f, spot, h], d, other(k))

    def pass_on(k, place, h, mask):
        ref = wg.at[source(k), place, h]
        return send(ref, ref, flip(d, mask), f)

    load_ctx.wait()
    for part in range(nf):
        ctx_t[part] = ctx[:, part * depth : (part + 1) * depth].T
    ctx_all[core, f] = ctx_t[f]
    own.wait()
    load_res.wait()

    tile = 256

    def project(shard, first):
        def step(n, carry):
            cols = pl.ds(pl.multiple_of(n * tile, tile), tile)
            left = ctx[:, pl.ds(pl.multiple_of(shard * depth, 128), depth)]
            right = wg[shard, :, :, :, cols].reshape(depth, tile)
            before = res[:, cols].astype(F32) if first else hid[:, cols]
            hid[:, cols] = before + jnp.dot(left, right, preferred_element_type=F32)
            return carry

        lax.fori_loop(0, width // tile, step, 0)

    project(f, True)

    from_y, from_z, from_core = {}, {}, []
    for h in range(2):
        for k in range(1, nf):
            direct[h, k].wait_recv()
            from_y[h, k] = pass_on(k, spot, h, 2)
            from_z[h, k] = pass_on(k, spot, h, 4)
            from_core.append(pass_on(k, spot, h, 1))
    near_y, near_z, far = flip(spot, 2), flip(spot, 4), flip(spot, 6)
    ctx_copies = [
        send(ctx_t.at[other(k)], ctx_all.at[core, f], d, other(k)) for k in range(1, nf)
    ]
    sibling_ctx = [send(ctx_all.at[core, f], ctx_all.at[core, f], flip(d, 1), f)]
    across_y, across_z = {}, {}
    for k in range(1, nf):
        from_z[0, k].wait_recv()
        across_y[k] = pass_on(k, near_z, 0, 2)
        from_core.append(pass_on(k, near_z, 0, 1))
    for k in range(1, nf):
        from_y[0, k].wait_recv()
        from_core.append(pass_on(k, near_y, 0, 1))
    for k in range(1, nf):
        from_y[1, k].wait_recv()
        across_z[k] = pass_on(k, near_y, 1, 4)
        from_core.append(pass_on(k, near_y, 1, 1))
    for k in range(1, nf):
        from_z[1, k].wait_recv()
        from_core.append(pass_on(k, near_z, 1, 1))
    for k in range(1, nf):
        across_y[k].wait_recv()
        from_core.append(pass_on(k, far, 0, 1))
    for k in range(1, nf):
        across_z[k].wait_recv()
        from_core.append(pass_on(k, far, 1, 1))
    for copy in from_core:
        copy.wait_recv()
    for k in range(1, nf):
        project(source(k), False)

    gain = gain_ref[...].astype(F32)
    pooled_rows = []
    for s in range(2 * seqs):
        rows = slice(s * length, (s + 1) * length)
        h_rows = hid[rows, :]
        inv = lax.rsqrt(jnp.mean(h_rows * h_rows, axis=1, keepdims=True) + 1e-05)
        invs[rows, :] = jnp.broadcast_to(inv, (length, invs.shape[1]))
        pooled_rows.append(jnp.sum(h_rows * inv, axis=0, keepdims=True))
    pooled = jnp.concatenate(pooled_rows, axis=0) * (gain / length)
    scale = lax.rsqrt(jnp.sum(pooled * pooled, axis=1, keepdims=True) + 1e-06)
    unit = pooled * scale

    per = 2 * seqs
    folds = 16 // per
    fold = width // folds
    lanes = msg.shape[1] - fold
    folded = jnp.concatenate([unit[:, i * fold : (i + 1) * fold] for i in range(folds)], axis=0)
    pattern = jnp.broadcast_to(pattern_ref[...].astype(F32), (16, nd)).astype(BF16)
    allowed_row = jnp.dot(pattern, spread_ref[...], preferred_element_type=F32)
    row_id = lax.broadcasted_iota(jnp.int32, (16, lanes), 0)
    lane_id = lax.broadcasted_iota(jnp.int32, (16, lanes), 1)
    meta = jnp.where(row_id < seqs, allowed_row, 0.0)
    for s in range(seqs):
        hit = jnp.logical_and(row_id == seqs + s, lane_id == positive_ref[s : s + 1, :] + d * seqs)
        meta = jnp.where(hit, 1.0, meta)
    msg[:, :fold] = folded.astype(BF16)
    msg[:, fold:] = meta.astype(BF16)
    pool_copies = [
        send(msg, pool.at[d], lax.rem(d + s, nd), f) for s in range(1, nd)
    ]
    pool[d] = msg[...]
    for k in range(1, nf):
        ctx_copies[k - 1].wait_recv()
        ref = ctx_all.at[core, source(k)]
        sibling_ctx.append(send(ref, ref, flip(d, 1), f))
    for copy in pool_copies:
        copy.wait_recv()

    cols = nd * seqs
    x = pool[:, :, :fold].reshape(nd * 16, fold)
    info = pool[:, :, fold:].reshape(nd * 16, lanes)
    pick_q = select_ref[:cols, :]
    pick_p = select_ref[cols:, :]
    same = same_ref[...]
    gram = lax.dot_general(x, x, NT, preferred_element_type=F32) * same
    half = jnp.dot(pick_q, gram, preferred_element_type=F32, precision=HIGH)
    scores = 20.0 * lax.dot_general(
        half, pick_p, NT, preferred_element_type=F32, precision=HIGH
    )
    allowed = jnp.dot(pick_q.astype(BF16), info, preferred_element_type=F32)[:, :cols]
    onehot = jnp.dot(pick_p.astype(BF16), info, preferred_element_type=F32)[:, :cols]
    weighted = allowed * jnp.exp(scores)
    total = jnp.sum(weighted, axis=1, keepdims=True)
    losses = jnp.log(total) - jnp.sum(onehot * scores, axis=1, keepdims=True)
    coeff = (weighted / total - onehot).astype(BF16)
    col_id = lax.broadcasted_iota(jnp.int32, (cols, 1), 0)
    for s in range(seqs):
        loss_ref[s : s + 1, :] = jnp.sum(
            jnp.where(col_id == d * seqs + s, losses, 0.0), axis=0, keepdims=True
        )
    lane_col = lax.broadcasted_iota(jnp.int32, (16, cols), 1) - d * seqs
    mine_q = jnp.where(lane_col == rows_ref[0], 1.0, 0.0).astype(BF16)
    mine_p = jnp.where(lane_col == rows_ref[1], 1.0, 0.0).astype(BF16)
    coeff_q = jnp.dot(mine_q, coeff, preferred_element_type=F32).astype(BF16)
    coeff_p = lax.dot_general(mine_p, coeff, NT, preferred_element_type=F32).astype(BF16)
    mix = jnp.dot(coeff_q, pick_p.astype(BF16), preferred_element_type=F32)
    mix = mix + jnp.dot(coeff_p, pick_q.astype(BF16), preferred_element_type=F32)
    mix = (mix * same[:16, :]).astype(BF16)
    d_fold = 20.0 * jnp.dot(mix, x, preferred_element_type=F32)
    d_embed = jnp.concatenate([d_fold[i * per : (i + 1) * per, :] for i in range(folds)], axis=1)
    d_pooled = (d_embed - unit * jnp.sum(unit * d_embed, axis=1, keepdims=True)) * scale
    d_gated = d_pooled * (gain / length)

    for s in range(2 * seqs):
        rows = slice(s * length, (s + 1) * length)
        h_rows = hid[rows, :]
        inv = invs[rows, 0:1]
        gated = d_gated[s : s + 1, :]
        mean = jnp.mean(h_rows * gated, axis=1, keepdims=True)
        d_rows = inv * gated - h_rows * (inv * inv * inv * mean)
        for i in range(nz):
            for j in range(2):
                first = (4 * i + j) * bw
                second = (4 * i + 2 + j) * bw
                pair = [d_rows[:, first : first + bw], d_rows[:, second : second + bw]]
                dhs[j, i, rows, :] = jnp.concatenate(pair, axis=1).astype(BF16)

    masks = list(range(nz - 1, -1, -1))
    peers = [(dc, k) for dc in range(2) for k in range(nf) if (dc, k) != (0, 0)]
    dh_copies = {}
    for mask in masks:
        block = flip(z, mask)
        for dc, k in peers:
            dh_copies[mask, dc, k] = send(
                dhs.at[flip(core, dc), block],
                dh_all.at[core, f, block],
                flip(d, dc),
                other(k),
            )
    for copy in sibling_ctx:
        copy.wait_recv()

    row_tile = min(256, depth)
    y_copies, z_copies = {}, []

    def reduce_block(mask):
        block = flip(z, mask)
        for dc, k in peers:
            dh_copies[mask, dc, k].wait_recv()

        def step(n, carry):
            at = pl.ds(pl.multiple_of(n * row_tile, row_tile), row_tile)
            total = jnp.dot(ctx_all[core, f, at, :], dhs[core, block], preferred_element_type=F32)
            for dc, k in peers:
                a, b = flip(core, dc), source(k)
                total += jnp.dot(
                    ctx_all[a, b, at, :], dh_all[a, b, block], preferred_element_type=F32
                )
            low, high = total[:, :bw], total[:, bw:]
            y_send[mask, at, :] = jnp.where(y == 0, high, low).astype(BF16)
            kept[mask, at, :] = jnp.where(y == 0, low, high)
            return carry

        lax.fori_loop(0, depth // row_tile, step, 0)
        y_copies[mask] = send(y_send.at[mask], y_recv.at[mask], flip(d, 2), f)

    def forward_block(mask):
        y_copies[mask].wait_recv()
        z_send[mask] = (kept[mask] + y_recv[mask].astype(F32)).astype(BF16)
        z_copies.append(send(z_send.at[mask], z_recv.at[mask], flip(d, 4 * mask), f))

    for place, mask in enumerate(masks):
        reduce_block(mask)
        if place:
            forward_block(masks[place - 1])
    y_copies[0].wait_recv()
    grad = kept[0] + y_recv[0].astype(F32)
    for place, copy in enumerate(z_copies):
        copy.wait_recv()
        grad = grad + z_recv[masks[place]].astype(F32)
    grad_ref[...] = grad
    for copy in started:
        copy.wait_send()


def body(nd, nf, context, residual, weight, gain, pattern, positive):
    tokens, width = context.shape
    depth = weight.shape[0]
    seqs = positive.shape[0]
    nz = nd // 4
    bw = width // nd
    per = 2 * seqs
    folds = 16 // per
    fold = width // folds
    lanes = 128
    cols = nd * seqs
    flat = np.arange(nd * 16)
    col = np.arange(cols)[:, None]
    owner = flat[None, :] // 16 == col // seqs
    pick_q = owner & (flat[None, :] % per == col % seqs)
    pick_p = owner & (flat[None, :] % per == seqs + col % seqs)
    select = np.concatenate([pick_q, pick_p]).astype(np.float32)
    group = (flat % 16) // per
    same = (group[:, None] == group[None, :]).astype(np.float32)
    spread = (np.arange(lanes)[None, :] // seqs == np.arange(nd)[:, None]).astype(np.float32)
    row = np.broadcast_to((np.arange(16) % per)[:, None], (16, cols))
    rows = np.stack([np.where(row < seqs, row, -4096), np.where(row >= seqs, row - seqs, -4096)])
    vmem = pl.BlockSpec(memory_space=pltpu.VMEM)
    hbm = pl.BlockSpec(memory_space=pl.ANY)
    copies = count_copies(nd, nf)
    losses, grad = pl.pallas_call(
        functools.partial(kernel, nd, nf, seqs),
        out_shape=(
            jax.ShapeDtypeStruct((seqs, 1), F32),
            jax.ShapeDtypeStruct((depth, bw), F32),
        ),
        in_specs=[hbm, hbm, hbm] + [vmem] * 7,
        out_specs=(vmem, vmem),
        scratch_shapes=[
            pltpu.VMEM((tokens, width), BF16),
            pltpu.VMEM((tokens, width), BF16),
            pltpu.VMEM((nf, 8, 2, depth // 16, width), BF16),
            pltpu.VMEM((tokens, width), F32),
            pltpu.VMEM((tokens, 128), F32),
            pltpu.VMEM((nf, depth, tokens), BF16),
            pltpu.VMEM((2, nf, depth, tokens), BF16),
            pltpu.VMEM((16, fold + lanes), BF16),
            pltpu.VMEM((nd, 16, fold + lanes), BF16),
            pltpu.VMEM((2, nz, tokens, 2 * bw), BF16),
            pltpu.VMEM((2, nf, nz, tokens, 2 * bw), BF16),
            pltpu.VMEM((nz, depth, bw), BF16),
            pltpu.VMEM((nz, depth, bw), BF16),
            pltpu.VMEM((nz, depth, bw), F32),
            pltpu.VMEM((nz, depth, bw), BF16),
            pltpu.VMEM((nz, depth, bw), BF16),
            pltpu.SemaphoreType.DMA((3,)),
            pltpu.SemaphoreType.DMA((copies,)),
            pltpu.SemaphoreType.DMA((copies,)),
        ],
        compiler_params=pltpu.CompilerParams(
            collective_id=0, has_side_effects=True, vmem_limit_bytes=52 * 1024 * 1024
        ),
        cost_estimate=pl.CostEstimate(
            flops=8 * tokens * width * width, bytes_accessed=8 * depth * width, transcendentals=0
        ),
    )(
        context,
        residual,
        weight.reshape(8, 2, depth // 16, width),
        gain.reshape(1, width),
        pattern,
        positive.reshape(seqs, 1),
        jnp.asarray(spread, BF16),
        jnp.asarray(select),
        jnp.asarray(same),
        jnp.asarray(rows, jnp.int32),
    )
    return losses.reshape(seqs), grad


def solution(mesh):
    return jax.shard_map(
        functools.partial(body, mesh.shape["dp"], mesh.shape["fsdp"]),
        mesh=mesh,
        in_specs=(
            P(("dp", "fsdp"), None),
            P(("dp", "fsdp"), None),
            P("fsdp", None),
            P(),
            P(("dp", "fsdp"), None),
            P(("dp", "fsdp")),
        ),
        out_specs=(P(("dp", "fsdp")), P("fsdp", "dp")),
        check_vma=False,
    )
```

time: 451 us -> 98.2 us (0.22)
  waiting for transfers between devices: 393 us -> 0 us
  Pallas kernels: 0 us -> 89.2 us
  blocking collectives: 21.7 us -> 0 us
  matrix products: 15.7 us -> 0 us
  between operations: 14.6 us -> 0.65 us
    reduce_scatter x2 -> x0, waiting for transfers between devices: 200 us -> none  [the longest x1 179 us: body(): lax.psum_scatter(lax.dot_general(columns, context, (((0,), (0,)), ((), ()...]
    all_gather x1 -> x0, waiting for transfers between devices: 107 us -> none  [body(): lax.all_gather(weight, 'fsdp', axis=0, tiled=True)]
    pallas_call x0 -> x1, Pallas kernels: none -> 89.2 us  [body(): pl.pallas_call(functools.partial(kernel, nd, nf, seqs), out_shape=(jax.Sh...]
    unnamed x5 -> x0, waiting for transfers between devices: 85.7 us -> none
    all_gather x1 -> x0, blocking collectives: 21.7 us -> none  [body(): pool = lax.all_gather(premise, 'dp', axis=0, tiled=True)]
    dot_general x5 -> x0, matrix products: 15.7 us -> none  [the longest x1 8.1 us: body(): lax.dot_general(columns, context, (((0,), (0,)), ((), ())), preferred_ele...]
  transfers between devices with their start and end apart: 4 -> 0, of which waited for: 4 -> 0; matrix products, arithmetic and copies ran while one was open for 0% -> 0% of each run, Pallas kernels for 0% -> 0%
where the time goes in v1:
time: 98.2 us; the launch traced here: 97.8 us
  Pallas kernels  89.2 us (91%)
  local copies, waits for them, and re-layouts  7.3 us (7%)
    pallas_call x1, Pallas kernels, body(): pl.pallas_call(functools.partial(kernel, nd, nf, seqs), out_shape=(jax.Sh...  89.2 us
    unnamed x13, local copies, waits for them, and re-layouts  5.86 us

profile of v1, /device:TPU:0, one launch (start us, length us, event | category | flops | bytes accessed | tf_op | source)
XLA Modules:
  0.0 97.8 jit_solution(5574772225523307452)
XLA Ops:
  0.6 0.7 copy.13.positive_ref
  1.4 0.7 reshape.17.gain_ref
  2.1 0.0 copy-start
  2.1 1.2 %copy-done = bf16[256,2048]{1,0:T(8,128)(2,1)S(1)} copy-done((bf16[256,2048]{1,0:T(8,128)(2,1)S(1)}, bf16[256,2048]{1,0:T(8,128)(2,1)}, u32[]{:S(2)}) %copy-start) | copy-done | bytes 1048600
  3.3 0.0 copy-start.1
  3.3 0.7 copy-done.1
  3.9 0.0 copy-start.2
  3.9 0.9 copy-done.2
  4.9 0.0 copy-start.3
  4.9 0.8 copy-done.3
  5.7 0.0 copy-start.4
  5.7 0.7 copy-done.4
  6.5 0.0 copy-start.5
  6.5 0.7 copy-done.5
  7.1 89.2 %shard_map.113 = (f32[2,1]{1,0:T(2,128)S(1)}, f32[1024,128]{1,0:T(8,128)S(1)}) custom-call(bf16[256,2048]{1,0:T(8,128)(2,1)S(1)} %copy-done, bf16[256,2048]{1,0:T(8,128)(2,1)} %residual_hbm.1, bf16[8,2,64,2048]{3,2,1,0:T(8,128)(2,1)} %bitcast.2, bf16[1,2048]{1,0:T(2,128)(2,1)S(1)} %reshape.17.gain_ref, s32[1,16]{1,0:T(1,128)S(1)} %copy-done.1, ...), custom_call_target="tpu_custom_call" | custom-call | flops 8589934592 | bytes 16777216 | tf_op jit(solution)/shard_map/pallas_call | solution.py:353
  96.4 0.6 reduce
  97.0 0.8 copy.15
Async XLA Ops:
  2.1 1.2 %copy-start = (bf16[256,2048]{1,0:T(8,128)(2,1)S(1)}, bf16[256,2048]{1,0:T(8,128)(2,1)}, u32[]{:S(2)}) copy-start(bf16[256,2048]{1,0:T(8,128)(2,1)} %context_hbm.1) | copy-start | bytes 3145732
  3.3 0.7 copy-start.1
  3.9 0.9 copy-start.2
  4.9 0.8 copy-start.3
  5.7 0.7 copy-start.4
  6.5 0.7 copy-start.5

commit v2 on v1

v2 whole, which is shorter than its diff:
```python
import functools

import jax
import jax.numpy as jnp
from jax import lax
from jax.experimental import pallas as pl
from jax.experimental.pallas import tpu as pltpu
from jax.sharding import PartitionSpec as P

MESH = pl.DeviceIdType.MESH
F32 = jnp.float32
BF16 = jnp.bfloat16
HIGH = lax.Precision.HIGHEST
NT = (((1,), (1,)), ((), ()))


def flip(index, mask):
    out = index
    bit = 1
    while bit <= mask:
        if mask & bit:
            out = out + bit * (1 - 2 * lax.rem(lax.div(index, bit), 2))
        bit *= 2
    return out


def count_copies(nd, nf):
    nz = nd // 4
    groups = nd // 2
    weights = (nf - 1) * (4 + 2 + 5 + 5 + 16)
    return weights + (nf - 1) + nf + 4 * groups + (2 * nf - 1) * nz + nz + nz - 1


def kernel(
    nd,
    nf,
    seqs,
    context_hbm,
    residual_hbm,
    weight_hbm,
    gain_hbm,
    pattern_hbm,
    positive_ref,
    loss_ref,
    grad_ref,
    ctx,
    res,
    gain_ref,
    pattern_ref,
    wg,
    hid,
    invs,
    ctx_t,
    ctx_all,
    note,
    notes,
    msg,
    pool,
    dhs,
    dh_all,
    y_send,
    y_recv,
    kept,
    z_send,
    z_recv,
    local_sem,
    send_sem,
    recv_sem,
):
    d = lax.axis_index("dp")
    f = lax.axis_index("fsdp")
    tokens, width = ctx.shape
    depth = wg.shape[1]
    nz = nd // 4
    bw = width // nd
    core = lax.rem(d, 2)
    y = lax.rem(lax.div(d, 2), 2)
    z = lax.div(d, 4)
    spot = lax.rem(d, 8)
    length = tokens // (2 * seqs)
    parts = 4
    rows_in = depth // 8
    wide = width // parts
    other = lambda k: lax.rem(f + k, nf)
    source = lambda k: lax.rem(f + nf - k, nf)
    others = range(1, nf)

    started = []

    def send(src, dst, dd, ff):
        slot = len(started)
        copy = pltpu.make_async_remote_copy(
            src_ref=src,
            dst_ref=dst,
            send_sem=send_sem.at[slot],
            recv_sem=recv_sem.at[slot],
            device_id=(dd, ff),
            device_id_type=MESH,
        )
        copy.start()
        started.append(copy)
        return copy

    def load(src, dst, slot):
        copy = pltpu.make_async_copy(src, dst, local_sem.at[slot])
        copy.start()
        return copy

    loads = [
        load(context_hbm, ctx, 0),
        load(weight_hbm, wg.at[f], 1),
        load(residual_hbm, res, 2),
        load(gain_hbm, gain_ref, 3),
        load(pattern_hbm, pattern_ref, 4),
    ]

    barrier = pltpu.get_barrier_semaphore()
    sibling = flip(d, 1)
    partners = [(lax.rem(d + 2 * s, nd), f) for s in range(1, nd // 2)] + [(sibling, f)]
    partners += [(d, other(k)) for k in others] + [(sibling, other(k)) for k in others]
    for partner in partners:
        pl.semaphore_signal(barrier, inc=1, device_id=partner, device_id_type=MESH)
    pl.semaphore_wait(barrier, len(partners))

    near_y, near_z, far = flip(spot, 2), flip(spot, 4), flip(spot, 6)

    def piece(place, h):
        return (pl.ds(pl.multiple_of(place * rows_in, rows_in), rows_in), slice(h * wide, (h + 1) * wide))

    def fetch(place, h):
        at = piece(place, h)
        return [send(weight_hbm.at[at], wg.at[(f, *at)], d, other(k)) for k in others]

    def pass_on(place, h, mask):
        at = piece(place, h)
        copies = []
        for k in others:
            ref = wg.at[(source(k), *at)]
            copies.append(send(ref, ref, flip(d, mask), f))
        return copies

    def arrive(copies):
        for copy in copies:
            copy.wait_recv()

    direct = {0: fetch(spot, 0), 1: fetch(spot, 1)}

    loads[4].wait()
    lanes = note.shape[1]
    lane_id = lax.broadcasted_iota(jnp.int32, (16, lanes), 1)
    row_id = lax.broadcasted_iota(jnp.int32, (16, lanes), 0)
    log_s = seqs.bit_length() - 1
    spread_lane = lax.broadcasted_iota(jnp.int32, (nd, lanes), 1) >> log_s
    spread = spread_lane == lax.broadcasted_iota(jnp.int32, (nd, lanes), 0)
    pattern = jnp.broadcast_to(pattern_ref[...].astype(F32), (16, nd)).astype(BF16)
    allowed_row = jnp.dot(
        pattern, jnp.where(spread, 1.0, 0.0).astype(BF16), preferred_element_type=F32
    )
    meta = jnp.where(row_id < seqs, allowed_row, 0.0)
    for s in range(seqs):
        hit = jnp.logical_and(row_id == seqs + s, lane_id == positive_ref[s] + d * seqs)
        meta = jnp.where(hit, 1.0, meta)
    note[...] = meta.astype(BF16)
    notes[d] = note[...]
    near = [lax.rem(d + 2 * s, nd) for s in range(1, nd // 2)]
    behind = [lax.rem(d + nd - 2 * s, nd) for s in range(1, nd // 2)]
    note_copies = [send(note, notes.at[d], there, f) for there in near]
    note_pairs = [send(note, notes.at[d], sibling, f)]

    loads[0].wait()
    for part in range(nf):
        ctx_t[part] = ctx[:, part * depth : (part + 1) * depth].T
    ctx_all[core, f] = ctx_t[f]
    sibling_ctx = [send(ctx_all.at[core, f], ctx_all.at[core, f], sibling, f)]
    loads[1].wait()
    loads[2].wait()
    tile = 256

    def project(shard, first, start, count):
        def step(n, carry):
            cols = pl.ds(pl.multiple_of(n * tile, tile), tile)
            left = ctx[:, pl.ds(pl.multiple_of(shard * depth, 128), depth)]
            before = res[:, cols].astype(F32) if first else hid[:, cols]
            hid[:, cols] = before + jnp.dot(left, wg[shard, :, cols], preferred_element_type=F32)
            return carry

        lax.fori_loop(start // tile, (start + count) // tile, step, 0)

    arrive(direct[0])
    to_y, to_z, to_core, straight = {}, {}, {h: [] for h in range(parts)}, {}

    def spread_out(h):
        to_y[h] = pass_on(spot, h, 2)
        to_z[h] = pass_on(spot, h, 4)
        to_core[h] += pass_on(spot, h, 1)

    def finish(h):
        arrive(to_core[h])
        for k in others:
            project(source(k), False, h * wide, wide)

    spread_out(0)
    direct[2], straight[2] = fetch(spot, 2), fetch(far, 2)
    project(f, True, 0, width)
    arrive(direct[1])
    spread_out(1)
    direct[3], straight[3] = fetch(spot, 3), fetch(far, 3)
    arrive(to_z[0])
    across_y = pass_on(near_z, 0, 2)
    to_core[0] += pass_on(near_z, 0, 1)
    arrive(to_y[0])
    to_core[0] += pass_on(near_y, 0, 1)
    arrive(direct[2])
    spread_out(2)
    arrive(to_y[1])
    across_z = pass_on(near_y, 1, 4)
    to_core[1] += pass_on(near_y, 1, 1)
    arrive(to_z[1])
    to_core[1] += pass_on(near_z, 1, 1)
    arrive(straight[2])
    to_core[2] += pass_on(far, 2, 1)
    arrive(across_y)
    to_core[0] += pass_on(far, 0, 1)
    arrive(direct[3])
    spread_out(3)
    ctx_copies = [send(ctx_t.at[other(k)], ctx_all.at[core, f], d, other(k)) for k in others]
    finish(0)
    arrive(across_z)
    to_core[1] += pass_on(far, 1, 1)
    arrive(to_y[2])
    to_core[2] += pass_on(near_y, 2, 1)
    arrive(to_z[2])
    to_core[2] += pass_on(near_z, 2, 1)
    arrive(straight[3])
    to_core[3] += pass_on(far, 3, 1)
    finish(1)
    finish(2)
    arrive(to_y[3])
    to_core[3] += pass_on(near_y, 3, 1)
    arrive(to_z[3])
    to_core[3] += pass_on(near_z, 3, 1)
    for copy, origin in zip(note_copies, behind):
        copy.wait_recv()
        note_pairs.append(send(notes.at[origin], notes.at[origin], sibling, f))
    finish(3)

    loads[3].wait()
    gain = gain_ref[...].astype(F32).reshape(1, width)
    pooled_rows = []
    for s in range(2 * seqs):
        rows = slice(s * length, (s + 1) * length)
        h_rows = hid[rows, :]
        inv = lax.rsqrt(jnp.mean(h_rows * h_rows, axis=1, keepdims=True) + 1e-05)
        invs[rows, :] = jnp.broadcast_to(inv, (length, invs.shape[1]))
        pooled_rows.append(jnp.sum(h_rows * inv, axis=0, keepdims=True))
    pooled = jnp.concatenate(pooled_rows, axis=0) * (gain / length)
    scale = lax.rsqrt(jnp.sum(pooled * pooled, axis=1, keepdims=True) + 1e-06)
    unit = pooled * scale
    per = 2 * seqs
    folds = 16 // per
    fold = width // folds
    folded = jnp.concatenate([unit[:, i * fold : (i + 1) * fold] for i in range(folds)], axis=0)
    msg[...] = folded.astype(BF16)
    pool_copies = [send(msg, pool.at[d], there, f) for there in near]
    pool_pairs = [send(msg, pool.at[d], sibling, f)]
    pool[d] = msg[...]

    cols = nd * seqs
    total_rows = nd * 16
    log_p = per.bit_length() - 1
    flat = lax.broadcasted_iota(jnp.int32, (cols, total_rows), 1)
    col = lax.broadcasted_iota(jnp.int32, (cols, total_rows), 0)
    owner = (flat >> 4) == (col >> log_s)
    inner, slot_in = flat & (per - 1), col & (seqs - 1)
    pick_q = jnp.where(jnp.logical_and(owner, inner == slot_in), 1.0, 0.0)
    pick_p = jnp.where(jnp.logical_and(owner, inner == slot_in + seqs), 1.0, 0.0)
    row_fold = (lax.broadcasted_iota(jnp.int32, (total_rows, total_rows), 0) & 15) >> log_p
    col_fold = (lax.broadcasted_iota(jnp.int32, (total_rows, total_rows), 1) & 15) >> log_p
    same = jnp.where(row_fold == col_fold, 1.0, 0.0)
    lane_col = lax.broadcasted_iota(jnp.int32, (16, cols), 1) - d * seqs
    row_in = lax.broadcasted_iota(jnp.int32, (16, cols), 0) & (per - 1)
    hit_q = jnp.logical_and(lane_col == row_in, row_in < seqs)
    hit_p = jnp.logical_and(lane_col + seqs == row_in, row_in >= seqs)
    mine_q = jnp.where(hit_q, 1.0, 0.0).astype(BF16)
    mine_p = jnp.where(hit_p, 1.0, 0.0).astype(BF16)
    arrive(note_pairs)
    info = notes[...].reshape(total_rows, lanes)
    allowed = jnp.dot(pick_q.astype(BF16), info, preferred_element_type=F32)[:, :cols]
    onehot = jnp.dot(pick_p.astype(BF16), info, preferred_element_type=F32)[:, :cols]

    for copy, origin in zip(pool_copies, behind):
        copy.wait_recv()
        pool_pairs.append(send(pool.at[origin], pool.at[origin], sibling, f))
    for k in others:
        ctx_copies[k - 1].wait_recv()
        ref = ctx_all.at[core, source(k)]
        sibling_ctx.append(send(ref, ref, sibling, f))
    arrive(pool_pairs)

    x = pool[...].reshape(total_rows, fold)
    gram = lax.dot_general(x, x, NT, preferred_element_type=F32) * same
    half = jnp.dot(pick_q, gram, preferred_element_type=F32, precision=HIGH)
    scores = 20.0 * lax.dot_general(
        half, pick_p, NT, preferred_element_type=F32, precision=HIGH
    )
    weighted = allowed * jnp.exp(scores)
    total = jnp.sum(weighted, axis=1, keepdims=True)
    losses = jnp.log(total) - jnp.sum(onehot * scores, axis=1, keepdims=True)
    coeff = (weighted / total - onehot).astype(BF16)
    coeff_q = jnp.dot(mine_q, coeff, preferred_element_type=F32).astype(BF16)
    coeff_p = lax.dot_general(mine_p, coeff, NT, preferred_element_type=F32).astype(BF16)
    mix = jnp.dot(coeff_q, pick_p.astype(BF16), preferred_element_type=F32)
    mix = mix + jnp.dot(coeff_p, pick_q.astype(BF16), preferred_element_type=F32)
    mix = (mix * same[:16, :]).astype(BF16)
    d_fold = 20.0 * jnp.dot(mix, x, preferred_element_type=F32)
    d_embed = jnp.concatenate([d_fold[i * per : (i + 1) * per, :] for i in range(folds)], axis=1)
    d_pooled = (d_embed - unit * jnp.sum(unit * d_embed, axis=1, keepdims=True)) * scale
    d_gated = d_pooled * (gain / length)

    for s in range(2 * seqs):
        rows = slice(s * length, (s + 1) * length)
        h_rows = hid[rows, :]
        inv = invs[rows, 0:1]
        gated = d_gated[s : s + 1, :]
        mean = jnp.mean(h_rows * gated, axis=1, keepdims=True)
        d_rows = inv * gated - h_rows * (inv * inv * inv * mean)
        for i in range(nz):
            for j in range(2):
                first = (4 * i + j) * bw
                second = (4 * i + 2 + j) * bw
                pair = [d_rows[:, first : first + bw], d_rows[:, second : second + bw]]
                dhs[j, i, rows, :] = jnp.concatenate(pair, axis=1).astype(BF16)

    masks = list(range(nz - 1, -1, -1))
    peers = [(dc, k) for dc in range(2) for k in range(nf) if (dc, k) != (0, 0)]
    dh_copies = {}

    def share(mask):
        block = flip(z, mask)
        for dc, k in peers:
            dh_copies[mask, dc, k] = send(
                dhs.at[flip(core, dc), block],
                dh_all.at[core, f, block],
                flip(d, dc),
                other(k),
            )

    for mask in masks[:2]:
        share(mask)
    col_id = lax.broadcasted_iota(jnp.int32, (cols, 1), 0)
    for s in range(seqs):
        loss_ref[s] = jnp.sum(jnp.where(col_id == d * seqs + s, losses, 0.0))
    arrive(sibling_ctx)

    row_tile = min(256, depth)
    y_copies, z_copies = {}, {}

    def reduce_block(place, mask):
        block = flip(z, mask)
        for dc, k in peers:
            dh_copies[mask, dc, k].wait_recv()
        if place + 2 < nz:
            share(masks[place + 2])

        def step(n, carry):
            at = pl.ds(pl.multiple_of(n * row_tile, row_tile), row_tile)
            total = jnp.dot(ctx_all[core, f, at, :], dhs[core, block], preferred_element_type=F32)
            for dc, k in peers:
                a, b = flip(core, dc), source(k)
                total += jnp.dot(
                    ctx_all[a, b, at, :], dh_all[a, b, block], preferred_element_type=F32
                )
            low, high = total[:, :bw], total[:, bw:]
            y_send[mask, at, :] = jnp.where(y == 0, high, low).astype(BF16)
            kept[mask, at, :] = jnp.where(y == 0, low, high)
            return carry

        lax.fori_loop(0, depth // row_tile, step, 0)
        y_copies[mask] = send(y_send.at[mask], y_recv.at[mask], flip(d, 2), f)

    def forward_block(mask):
        y_copies[mask].wait_recv()
        summed = kept[mask] + y_recv[mask].astype(F32)
        bit = 1
        while bit < nz and not mask & bit:
            z_copies[mask | bit].wait_recv()
            summed = summed + z_recv[mask | bit].astype(F32)
            bit *= 2
        if mask:
            z_send[mask] = summed.astype(BF16)
            z_copies[mask] = send(z_send.at[mask], z_recv.at[mask], flip(d, 4 * bit), f)
        else:
            grad_ref[...] = summed

    for place, mask in enumerate(masks):
        reduce_block(place, mask)
        if place:
            forward_block(masks[place - 1])
    forward_block(0)
    for copy in started:
        copy.wait_send()


def body(nd, nf, context, residual, weight, gain, pattern, positive):
    tokens, width = context.shape
    depth = weight.shape[0]
    seqs = positive.shape[0]
    nz = nd // 4
    bw = width // nd
    fold = width * 2 * seqs // 16
    lanes = 128
    vmem = pl.BlockSpec(memory_space=pltpu.VMEM)
    smem = pl.BlockSpec(memory_space=pltpu.SMEM)
    hbm = pl.BlockSpec(memory_space=pl.ANY)
    copies = count_copies(nd, nf)
    return pl.pallas_call(
        functools.partial(kernel, nd, nf, seqs),
        out_shape=(
            jax.ShapeDtypeStruct((seqs,), F32),
            jax.ShapeDtypeStruct((depth, bw), F32),
        ),
        in_specs=[hbm] * 5 + [smem],
        out_specs=(smem, vmem),
        scratch_shapes=[
            pltpu.VMEM((tokens, width), BF16),
            pltpu.VMEM((tokens, width), BF16),
            pltpu.VMEM((width,), BF16),
            pltpu.VMEM((1, nd), jnp.int32),
            pltpu.VMEM((nf, depth, width), BF16),
            pltpu.VMEM((tokens, width), F32),
            pltpu.VMEM((tokens, 128), F32),
            pltpu.VMEM((nf, depth, tokens), BF16),
            pltpu.VMEM((2, nf, depth, tokens), BF16),
            pltpu.VMEM((16, lanes), BF16),
            pltpu.VMEM((nd, 16, lanes), BF16),
            pltpu.VMEM((16, fold), BF16),
            pltpu.VMEM((nd, 16, fold), BF16),
            pltpu.VMEM((2, nz, tokens, 2 * bw), BF16),
            pltpu.VMEM((2, nf, nz, tokens, 2 * bw), BF16),
            pltpu.VMEM((nz, depth, bw), BF16),
            pltpu.VMEM((nz, depth, bw), BF16),
            pltpu.VMEM((nz, depth, bw), F32),
            pltpu.VMEM((nz, depth, bw), BF16),
            pltpu.VMEM((nz, depth, bw), BF16),
            pltpu.SemaphoreType.DMA((5,)),
            pltpu.SemaphoreType.DMA((copies,)),
            pltpu.SemaphoreType.DMA((copies,)),
        ],
        compiler_params=pltpu.CompilerParams(
            collective_id=0, has_side_effects=True, vmem_limit_bytes=52 * 1024 * 1024
        ),
        cost_estimate=pl.CostEstimate(
            flops=8 * tokens * width * width, bytes_accessed=8 * depth * width, transcendentals=0
        ),
    )(context, residual, weight, gain, pattern, positive)


def solution(mesh):
    return jax.shard_map(
        functools.partial(body, mesh.shape["dp"], mesh.shape["fsdp"]),
        mesh=mesh,
        in_specs=(
            P(("dp", "fsdp"), None),
            P(("dp", "fsdp"), None),
            P("fsdp", None),
            P(),
            P(("dp", "fsdp"), None),
            P(("dp", "fsdp")),
        ),
        out_specs=(P(("dp", "fsdp")), P("fsdp", "dp")),
        check_vma=False,
    )
```

time: 98.2 us -> 85.2 us (0.87)
  Pallas kernels: 89.2 us -> 79.8 us
  local copies, waits for them, and re-layouts: 7.3 us -> 4.52 us
    pallas_call x1, Pallas kernels: 89.2 us -> 79.8 us  [body(): pl.pallas_call(functools.partial(kernel, nd, nf, seqs), out_shape=(jax.Sh...]
    reshape x2 -> x0, local copies, waits for them, and re-layouts: 1.43 us -> none  [the longest x1 0.74 us: body(): positive.reshape(seqs, 1)]
    unnamed x13 -> x10, local copies, waits for them, and re-layouts: 5.86 us -> 4.52 us
where the time goes in v2:
time: 85.2 us; the launch traced here: 85 us
  Pallas kernels  79.8 us (94%)
  local copies, waits for them, and re-layouts  4.52 us (5%)
    pallas_call x1, Pallas kernels, body(): pl.pallas_call(functools.partial(kernel, nd, nf, seqs), out_shape=(jax.Sh...  79.8 us
    unnamed x10, local copies, waits for them, and re-layouts  4.52 us

profile of v2, /device:TPU:0, one launch (start us, length us, event | category | flops | bytes accessed | tf_op | source)
XLA Modules:
  0.0 85.0 jit_solution(11322035944404174526)
XLA Ops:
  0.6 0.0 copy-start
  0.6 1.2 %copy-done = bf16[256,2048]{1,0:T(8,128)(2,1)S(1)} copy-done((bf16[256,2048]{1,0:T(8,128)(2,1)S(1)}, bf16[256,2048]{1,0:T(8,128)(2,1)}, u32[]{:S(2)}) %copy-start) | copy-done | bytes 1048600
  1.9 0.0 copy-start.1
  1.9 0.7 copy-done.1
  2.5 0.0 copy-start.2
  2.5 0.7 copy-done.2
  3.2 0.0 copy-start.3
  3.2 0.7 copy-done.3
  3.9 79.8 %shard_map.77 = (f32[2]{0:T(128)S(1)}, f32[1024,128]{1,0:T(8,128)S(1)}) custom-call(bf16[256,2048]{1,0:T(8,128)(2,1)S(1)} %copy-done, bf16[256,2048]{1,0:T(8,128)(2,1)} %residual_hbm.1, bf16[1024,2048]{1,0:T(8,128)(2,1)} %weight_hbm.1, bf16[2048]{0:T(1024)(128)(2,1)S(1)} %copy-done.1, s32[1,16]{1,0:T(1,128)S(1)} %copy-done.2, s32[2]{0:T(128)S(1)} %copy-done.3), custom_call_target="tpu_custom_call" | custom-call | flops 8589934592 | bytes 16777216 | tf_op jit(solution)/shard_map/pallas_call | solution.py:416
  83.7 0.5 copy.10
  84.2 0.8 copy.11
Async XLA Ops:
  0.6 1.2 %copy-start = (bf16[256,2048]{1,0:T(8,128)(2,1)S(1)}, bf16[256,2048]{1,0:T(8,128)(2,1)}, u32[]{:S(2)}) copy-start(bf16[256,2048]{1,0:T(8,128)(2,1)} %context_hbm.1) | copy-start | bytes 3145732
  1.9 0.7 copy-start.1
  2.5 0.7 copy-start.2
  3.2 0.7 copy-start.3

commit v3 on v2

--- a/solution.py
+++ b/solution.py
@@ -28,7 +28,7 @@
     nz = nd // 4
     groups = nd // 2
     weights = (nf - 1) * (4 + 2 + 5 + 5 + 16)
-    return weights + (nf - 1) + nf + 4 * groups + (2 * nf - 1) * nz + nz + nz - 1
+    return weights + (nf - 1) + nf + 4 * groups + (2 * nf - 1) * (nz + 2) + nz + nz - 1
 
 
 def kernel(
@@ -40,13 +40,14 @@
     weight_hbm,
     gain_hbm,
     pattern_hbm,
-    positive_ref,
+    positive_hbm,
     loss_ref,
     grad_ref,
     ctx,
     res,
     gain_ref,
     pattern_ref,
+    positive_ref,
     wg,
     hid,
     invs,
@@ -56,8 +57,14 @@
     notes,
     msg,
     pool,
-    dhs,
-    dh_all,
+    hs,
+    hs_all,
+    gs,
+    gs_all,
+    tok,
+    tok_all,
+    weights,
+    dh,
     y_send,
     y_recv,
     kept,
@@ -112,6 +119,7 @@
         load(residual_hbm, res, 2),
         load(gain_hbm, gain_ref, 3),
         load(pattern_hbm, pattern_ref, 4),
+        load(positive_hbm, positive_ref, 5),
     ]
 
     barrier = pltpu.get_barrier_semaphore()
@@ -146,6 +154,7 @@
     direct = {0: fetch(spot, 0), 1: fetch(spot, 1)}
 
     loads[4].wait()
+    loads[5].wait()
     lanes = note.shape[1]
     lane_id = lax.broadcasted_iota(jnp.int32, (16, lanes), 1)
     row_id = lax.broadcasted_iota(jnp.int32, (16, lanes), 0)
@@ -198,6 +207,11 @@
         arrive(to_core[h])
         for k in others:
             project(source(k), False, h * wide, wide)
+        for i in range(h * nz // parts, (h + 1) * nz // parts):
+            for j in range(2):
+                first, second = (4 * i + j) * bw, (4 * i + 2 + j) * bw
+                pair = [hid[:, first : first + bw], hid[:, second : second + bw]]
+                hs[j, i] = jnp.concatenate(pair, axis=1).astype(BF16)
 
     spread_out(0)
     direct[2], straight[2] = fetch(spot, 2), fetch(far, 2)
@@ -244,6 +258,22 @@
         note_pairs.append(send(notes.at[origin], notes.at[origin], sibling, f))
     finish(3)
 
+    masks = list(range(nz - 1, -1, -1))
+    peers = [(dc, k) for dc in range(2) for k in range(nf) if (dc, k) != (0, 0)]
+    dh_copies = {}
+
+    def share(mask):
+        block = flip(z, mask)
+        for dc, k in peers:
+            dh_copies[mask, dc, k] = send(
+                hs.at[flip(core, dc), block],
+                hs_all.at[core, f, block],
+                flip(d, dc),
+                other(k),
+            )
+
+    share(masks[0])
+
     loads[3].wait()
     gain = gain_ref[...].astype(F32).reshape(1, width)
     pooled_rows = []
@@ -264,6 +294,7 @@
     pool_copies = [send(msg, pool.at[d], there, f) for there in near]
     pool_pairs = [send(msg, pool.at[d], sibling, f)]
     pool[d] = msg[...]
+    share(masks[1])
 
     cols = nd * seqs
     total_rows = nd * 16
@@ -296,6 +327,7 @@
         ref = ctx_all.at[core, source(k)]
         sibling_ctx.append(send(ref, ref, sibling, f))
     arrive(pool_pairs)
+    share(masks[2])
 
     x = pool[...].reshape(total_rows, fold)
     gram = lax.dot_general(x, x, NT, preferred_element_type=F32) * same
@@ -317,36 +349,25 @@
     d_pooled = (d_embed - unit * jnp.sum(unit * d_embed, axis=1, keepdims=True)) * scale
     d_gated = d_pooled * (gain / length)
 
+    for i in range(nz):
+        for j in range(2):
+            first, second = (4 * i + j) * bw, (4 * i + 2 + j) * bw
+            pair = [d_gated[:, first : first + bw], d_gated[:, second : second + bw]]
+            at = (i % 2) * 4
+            gs[j, i // 2, at : at + per, :] = jnp.concatenate(pair, axis=1)
+    gs_copies = {}
+    for dc, k in peers:
+        gs_copies[dc, k] = send(gs.at[flip(core, dc)], gs_all.at[core, f], flip(d, dc), other(k))
+    lane = lax.broadcasted_iota(jnp.int32, (length, 128), 1)
     for s in range(2 * seqs):
         rows = slice(s * length, (s + 1) * length)
-        h_rows = hid[rows, :]
         inv = invs[rows, 0:1]
-        gated = d_gated[s : s + 1, :]
-        mean = jnp.mean(h_rows * gated, axis=1, keepdims=True)
-        d_rows = inv * gated - h_rows * (inv * inv * inv * mean)
-        for i in range(nz):
-            for j in range(2):
-                first = (4 * i + j) * bw
-                second = (4 * i + 2 + j) * bw
-                pair = [d_rows[:, first : first + bw], d_rows[:, second : second + bw]]
-                dhs[j, i, rows, :] = jnp.concatenate(pair, axis=1).astype(BF16)
-
-    masks = list(range(nz - 1, -1, -1))
-    peers = [(dc, k) for dc in range(2) for k in range(nf) if (dc, k) != (0, 0)]
-    dh_copies = {}
-
-    def share(mask):
-        block = flip(z, mask)
-        for dc, k in peers:
-            dh_copies[mask, dc, k] = send(
-                dhs.at[flip(core, dc), block],
-                dh_all.at[core, f, block],
-                flip(d, dc),
-                other(k),
-            )
-
-    for mask in masks[:2]:
-        share(mask)
+        mean = jnp.mean(hid[rows, :] * d_gated[s : s + 1, :], axis=1, keepdims=True)
+        weights[0, rows, :] = jnp.where(lane < 4, inv, inv * inv * inv * mean)
+    tok[...] = weights[0].T[:8, :]
+    tok_copies = {}
+    for dc, k in peers:
+        tok_copies[dc, k] = send(tok, tok_all.at[core, f], flip(d, dc), other(k))
     col_id = lax.broadcasted_iota(jnp.int32, (cols, 1), 0)
     for s in range(seqs):
         loss_ref[s] = jnp.sum(jnp.where(col_id == d * seqs + s, losses, 0.0))
@@ -355,21 +376,37 @@
     row_tile = min(256, depth)
     y_copies, z_copies = {}, {}
 
+    for index, (dc, k) in enumerate(peers):
+        gs_copies[dc, k].wait_recv()
+        tok_copies[dc, k].wait_recv()
+        rows8 = tok_all[flip(core, dc), source(k)]
+        weights[index + 1] = jnp.concatenate([rows8] * 16, axis=0).T
+
+    def differentiate(index, h_block, gated, odd):
+        picked = jnp.where(odd == 1, gated[4 : 4 + per, :], gated[:per, :])
+        spread_rows = jnp.concatenate(
+            [jnp.broadcast_to(picked[s : s + 1, :], (length, 2 * bw)) for s in range(per)], axis=0
+        )
+        inv, slope = weights[index, :, 0:1], weights[index, :, 4:5]
+        dh[index] = (inv * spread_rows - h_block.astype(F32) * slope).astype(BF16)
+
     def reduce_block(place, mask):
         block = flip(z, mask)
-        for dc, k in peers:
+        half_block, odd = lax.div(block, 2), lax.rem(block, 2)
+        differentiate(0, hs[core, block], gs[core, half_block], odd)
+        for index, (dc, k) in enumerate(peers):
+            a, b = flip(core, dc), source(k)
             dh_copies[mask, dc, k].wait_recv()
-        if place + 2 < nz:
-            share(masks[place + 2])
+            differentiate(index + 1, hs_all[a, b, block], gs_all[a, b, half_block], odd)
+        if place + 3 < nz:
+            share(masks[place + 3])
 
         def step(n, carry):
             at = pl.ds(pl.multiple_of(n * row_tile, row_tile), row_tile)
-            total = jnp.dot(ctx_all[core, f, at, :], dhs[core, block], preferred_element_type=F32)
-            for dc, k in peers:
+            total = jnp.dot(ctx_all[core, f, at, :], dh[0], preferred_element_type=F32)
+            for index, (dc, k) in enumerate(peers):
                 a, b = flip(core, dc), source(k)
-                total += jnp.dot(
-                    ctx_all[a, b, at, :], dh_all[a, b, block], preferred_element_type=F32
-                )
+                total += jnp.dot(ctx_all[a, b, at, :], dh[index + 1], preferred_element_type=F32)
             low, high = total[:, :bw], total[:, bw:]
             y_send[mask, at, :] = jnp.where(y == 0, high, low).astype(BF16)
             kept[mask, at, :] = jnp.where(y == 0, low, high)
@@ -419,13 +456,14 @@
             jax.ShapeDtypeStruct((seqs,), F32),
             jax.ShapeDtypeStruct((depth, bw), F32),
         ),
-        in_specs=[hbm] * 5 + [smem],
+        in_specs=[hbm] * 6,
         out_specs=(smem, vmem),
         scratch_shapes=[
             pltpu.VMEM((tokens, width), BF16),
             pltpu.VMEM((tokens, width), BF16),
             pltpu.VMEM((width,), BF16),
             pltpu.VMEM((1, nd), jnp.int32),
+            pltpu.SMEM((seqs,), jnp.int32),
             pltpu.VMEM((nf, depth, width), BF16),
             pltpu.VMEM((tokens, width), F32),
             pltpu.VMEM((tokens, 128), F32),
@@ -437,17 +475,23 @@
             pltpu.VMEM((nd, 16, fold), BF16),
             pltpu.VMEM((2, nz, tokens, 2 * bw), BF16),
             pltpu.VMEM((2, nf, nz, tokens, 2 * bw), BF16),
+            pltpu.VMEM((2, nz // 2, 8, 2 * bw), F32),
+            pltpu.VMEM((2, nf, nz // 2, 8, 2 * bw), F32),
+            pltpu.VMEM((8, tokens), F32),
+            pltpu.VMEM((2, nf, 8, tokens), F32),
+            pltpu.VMEM((2 * nf, tokens, 128), F32),
+            pltpu.VMEM((2 * nf, tokens, 2 * bw), BF16),
             pltpu.VMEM((nz, depth, bw), BF16),
             pltpu.VMEM((nz, depth, bw), BF16),
             pltpu.VMEM((nz, depth, bw), F32),
             pltpu.VMEM((nz, depth, bw), BF16),
             pltpu.VMEM((nz, depth, bw), BF16),
-            pltpu.SemaphoreType.DMA((5,)),
+            pltpu.SemaphoreType.DMA((6,)),
             pltpu.SemaphoreType.DMA((copies,)),
             pltpu.SemaphoreType.DMA((copies,)),
         ],
         compiler_params=pltpu.CompilerParams(
-            collective_id=0, has_side_effects=True, vmem_limit_bytes=52 * 1024 * 1024
+            collective_id=0, has_side_effects=True, vmem_limit_bytes=63 * 1024 * 1024
         ),
         cost_estimate=pl.CostEstimate(
             flops=8 * tokens * width * width, bytes_accessed=8 * depth * width, transcendentals=0

time: 85.2 us -> 92.2 us (1.082)
  Pallas kernels: 79.8 us -> 88.4 us
  local copies, waits for them, and re-layouts: 4.52 us -> 2.97 us
    pallas_call x1, Pallas kernels: 79.8 us -> 88.4 us  [body(): pl.pallas_call(functools.partial(kernel, nd, nf, seqs), out_shape=(jax.Sh...]
    unnamed x10 -> x2, local copies, waits for them, and re-layouts: 4.52 us -> 2.97 us
where the time goes in v3:
time: 92.2 us; the launch traced here: 92.1 us
  Pallas kernels  88.4 us (96%)
  local copies, waits for them, and re-layouts  2.97 us (3%)
    pallas_call x1, Pallas kernels, body(): pl.pallas_call(functools.partial(kernel, nd, nf, seqs), out_shape=(jax.Sh...  88.4 us
    unnamed x2, local copies, waits for them, and re-layouts  2.97 us

profile of v3, /device:TPU:0, one launch (start us, length us, event | category | flops | bytes accessed | tf_op | source)
XLA Modules:
  0.0 92.1 jit_solution(2202057431933945075)
XLA Ops:
  0.6 88.4 %shard_map.77 = (f32[2]{0:T(128)}, f32[1024,128]{1,0:T(8,128)}) custom-call(bf16[256,2048]{1,0:T(8,128)(2,1)} %context_hbm.1, bf16[256,2048]{1,0:T(8,128)(2,1)} %residual_hbm.1, bf16[1024,2048]{1,0:T(8,128)(2,1)} %weight_hbm.1, bf16[2048]{0:T(1024)(128)(2,1)} %gain_hbm.1, s32[1,16]{1,0:T(1,128)} %pattern_hbm.1, s32[2]{0:T(128)} %positive_hbm.1), custom_call_target="tpu_custom_call" | custom-call | flops 8589934592 | bytes 16777216 | tf_op jit(solution)/shard_map/pallas_call | solution.py:453
  89.1 1.1 %copy.10 = f32[2]{0:T(128)} copy(f32[2]{0:T(128)} %get-tuple-element.4) | data formatting | bytes 16
  90.2 1.9 %copy.11 = f32[1024,128]{1,0:T(8,128)} copy(f32[1024,128]{1,0:T(8,128)} %get-tuple-element.5) | data formatting | bytes 1048576

commit v4 on v2

--- a/solution.py
+++ b/solution.py
@@ -28,7 +28,7 @@
     nz = nd // 4
     groups = nd // 2
     weights = (nf - 1) * (4 + 2 + 5 + 5 + 16)
-    return weights + (nf - 1) + nf + 4 * groups + (2 * nf - 1) * nz + nz + nz - 1
+    return weights + 16 * (nf - 1) + 1 + 4 * groups + (2 * nf - 1) * nz + nz + nz - 1
 
 
 def kernel(
@@ -50,6 +50,8 @@
     wg,
     hid,
     invs,
+    slopes,
+    g_rows,
     ctx_t,
     ctx_all,
     note,
@@ -199,6 +201,23 @@
         for k in others:
             project(source(k), False, h * wide, wide)
 
+    chunks = 8
+    ctx_copies = {}
+
+    def chunk(i):
+        return slice(i * depth // chunks, (i + 1) * depth // chunks)
+
+    def trickle(i):
+        for k in others:
+            src, dst = ctx_t.at[other(k), chunk(i)], ctx_all.at[core, f, chunk(i)]
+            ctx_copies[i, k] = send(src, dst, d, other(k))
+
+    def relay(i):
+        for k in others:
+            ctx_copies[i, k].wait_recv()
+            ref = ctx_all.at[core, source(k), chunk(i)]
+            sibling_ctx.append(send(ref, ref, sibling, f))
+
     spread_out(0)
     direct[2], straight[2] = fetch(spot, 2), fetch(far, 2)
     project(f, True, 0, width)
@@ -223,8 +242,9 @@
     to_core[0] += pass_on(far, 0, 1)
     arrive(direct[3])
     spread_out(3)
-    ctx_copies = [send(ctx_t.at[other(k)], ctx_all.at[core, f], d, other(k)) for k in others]
+    trickle(0)
     finish(0)
+    trickle(1)
     arrive(across_z)
     to_core[1] += pass_on(far, 1, 1)
     arrive(to_y[2])
@@ -233,7 +253,9 @@
     to_core[2] += pass_on(near_z, 2, 1)
     arrive(straight[3])
     to_core[3] += pass_on(far, 3, 1)
+    trickle(2)
     finish(1)
+    trickle(3)
     finish(2)
     arrive(to_y[3])
     to_core[3] += pass_on(near_y, 3, 1)
@@ -242,6 +264,7 @@
     for copy, origin in zip(note_copies, behind):
         copy.wait_recv()
         note_pairs.append(send(notes.at[origin], notes.at[origin], sibling, f))
+    trickle(4)
     finish(3)
 
     loads[3].wait()
@@ -291,10 +314,10 @@
     for copy, origin in zip(pool_copies, behind):
         copy.wait_recv()
         pool_pairs.append(send(pool.at[origin], pool.at[origin], sibling, f))
-    for k in others:
-        ctx_copies[k - 1].wait_recv()
-        ref = ctx_all.at[core, source(k)]
-        sibling_ctx.append(send(ref, ref, sibling, f))
+    for i in range(5, 8):
+        trickle(i)
+    for i in range(5):
+        relay(i)
     arrive(pool_pairs)
 
     x = pool[...].reshape(total_rows, fold)
@@ -317,19 +340,22 @@
     d_pooled = (d_embed - unit * jnp.sum(unit * d_embed, axis=1, keepdims=True)) * scale
     d_gated = d_pooled * (gain / length)
 
-    for s in range(2 * seqs):
+    g_rows[0:per, :] = d_gated
+    for s in range(per):
         rows = slice(s * length, (s + 1) * length)
-        h_rows = hid[rows, :]
         inv = invs[rows, 0:1]
-        gated = d_gated[s : s + 1, :]
-        mean = jnp.mean(h_rows * gated, axis=1, keepdims=True)
-        d_rows = inv * gated - h_rows * (inv * inv * inv * mean)
-        for i in range(nz):
+        mean = jnp.mean(hid[rows, :] * d_gated[s : s + 1, :], axis=1, keepdims=True)
+        slopes[rows, :] = jnp.broadcast_to(inv * inv * inv * mean, (length, slopes.shape[1]))
+
+    def differentiate(block):
+        at = pl.ds(pl.multiple_of(block * 4 * bw, 128), 4 * bw)
+        for s in range(per):
+            rows = slice(s * length, (s + 1) * length)
+            inv, slope = invs[rows, 0:1], slopes[rows, 0:1]
+            d_rows = inv * g_rows[s : s + 1, at] - hid[rows, at] * slope
             for j in range(2):
-                first = (4 * i + j) * bw
-                second = (4 * i + 2 + j) * bw
-                pair = [d_rows[:, first : first + bw], d_rows[:, second : second + bw]]
-                dhs[j, i, rows, :] = jnp.concatenate(pair, axis=1).astype(BF16)
+                pair = [d_rows[:, j * bw : (j + 1) * bw], d_rows[:, (2 + j) * bw : (3 + j) * bw]]
+                dhs[j, block, rows, :] = jnp.concatenate(pair, axis=1).astype(BF16)
 
     masks = list(range(nz - 1, -1, -1))
     peers = [(dc, k) for dc in range(2) for k in range(nf) if (dc, k) != (0, 0)]
@@ -345,8 +371,12 @@
                 other(k),
             )
 
-    for mask in masks[:2]:
-        share(mask)
+    for place, mask in enumerate(masks):
+        differentiate(flip(z, mask))
+        if place < 2:
+            share(mask)
+    for i in range(5, 8):
+        relay(i)
     col_id = lax.broadcasted_iota(jnp.int32, (cols, 1), 0)
     for s in range(seqs):
         loss_ref[s] = jnp.sum(jnp.where(col_id == d * seqs + s, losses, 0.0))
@@ -429,6 +459,8 @@
             pltpu.VMEM((nf, depth, width), BF16),
             pltpu.VMEM((tokens, width), F32),
             pltpu.VMEM((tokens, 128), F32),
+            pltpu.VMEM((tokens, 128), F32),
+            pltpu.VMEM((8, width), F32),
             pltpu.VMEM((nf, depth, tokens), BF16),
             pltpu.VMEM((2, nf, depth, tokens), BF16),
             pltpu.VMEM((16, lanes), BF16),
@@ -447,7 +479,7 @@
             pltpu.SemaphoreType.DMA((copies,)),
         ],
         compiler_params=pltpu.CompilerParams(
-            collective_id=0, has_side_effects=True, vmem_limit_bytes=52 * 1024 * 1024
+            collective_id=0, has_side_effects=True, vmem_limit_bytes=63 * 1024 * 1024
         ),
         cost_estimate=pl.CostEstimate(
             flops=8 * tokens * width * width, bytes_accessed=8 * depth * width, transcendentals=0

time: 85.2 us -> 84.6 us (level)
  local copies, waits for them, and re-layouts: 4.52 us -> 2.97 us
  Pallas kernels: 79.8 us -> 80.8 us
    unnamed x10 -> x2, local copies, waits for them, and re-layouts: 4.52 us -> 2.97 us
    pallas_call x1, Pallas kernels: 79.8 us -> 80.8 us  [body(): pl.pallas_call(functools.partial(kernel, nd, nf, seqs), out_shape=(jax.Sh...]
where the time goes in v4:
time: 84.6 us; the launch traced here: 84.4 us
  Pallas kernels  80.8 us (96%)
  local copies, waits for them, and re-layouts  2.97 us (4%)
    pallas_call x1, Pallas kernels, body(): pl.pallas_call(functools.partial(kernel, nd, nf, seqs), out_shape=(jax.Sh...  80.8 us
    unnamed x2, local copies, waits for them, and re-layouts  2.97 us

profile of v4, /device:TPU:0, one launch (start us, length us, event | category | flops | bytes accessed | tf_op | source)
XLA Modules:
  0.0 84.4 jit_solution(10918430927307928209)
XLA Ops:
  0.6 80.8 %shard_map.77 = (f32[2]{0:T(128)}, f32[1024,128]{1,0:T(8,128)}) custom-call(bf16[256,2048]{1,0:T(8,128)(2,1)} %context_hbm.1, bf16[256,2048]{1,0:T(8,128)(2,1)} %residual_hbm.1, bf16[1024,2048]{1,0:T(8,128)(2,1)} %weight_hbm.1, bf16[2048]{0:T(1024)(128)(2,1)} %gain_hbm.1, s32[1,16]{1,0:T(1,128)} %pattern_hbm.1, s32[2]{0:T(128)} %positive_ref.1), custom_call_target="tpu_custom_call" | custom-call | flops 8589934592 | bytes 16777216 | tf_op jit(solution)/shard_map/pallas_call | solution.py:446
  81.4 1.1 %copy.10 = f32[2]{0:T(128)} copy(f32[2]{0:T(128)} %get-tuple-element.4) | data formatting | bytes 16
  82.6 1.9 %copy.11 = f32[1024,128]{1,0:T(8,128)} copy(f32[1024,128]{1,0:T(8,128)} %get-tuple-element.5) | data formatting | bytes 1048576

commit v5 on v4

--- a/solution.py
+++ b/solution.py
@@ -10,7 +10,6 @@
 MESH = pl.DeviceIdType.MESH
 F32 = jnp.float32
 BF16 = jnp.bfloat16
-HIGH = lax.Precision.HIGHEST
 NT = (((1,), (1,)), ((), ()))
 
 
@@ -28,7 +27,7 @@
     nz = nd // 4
     groups = nd // 2
     weights = (nf - 1) * (4 + 2 + 5 + 5 + 16)
-    return weights + 16 * (nf - 1) + 1 + 4 * groups + (2 * nf - 1) * nz + nz + nz - 1
+    return weights + 16 * (nf - 1) + 1 + 4 * groups + (2 * nf - 1) * 2 * nz + nz + nz - 1
 
 
 def kernel(
@@ -145,7 +144,7 @@
         for copy in copies:
             copy.wait_recv()
 
-    direct = {0: fetch(spot, 0), 1: fetch(spot, 1)}
+    direct = {0: fetch(spot, 0)}
 
     loads[4].wait()
     lanes = note.shape[1]
@@ -172,6 +171,7 @@
     loads[0].wait()
     for part in range(nf):
         ctx_t[part] = ctx[:, part * depth : (part + 1) * depth].T
+    direct[1] = fetch(spot, 1)
     ctx_all[core, f] = ctx_t[f]
     sibling_ctx = [send(ctx_all.at[core, f], ctx_all.at[core, f], sibling, f)]
     loads[1].wait()
@@ -295,8 +295,8 @@
     col = lax.broadcasted_iota(jnp.int32, (cols, total_rows), 0)
     owner = (flat >> 4) == (col >> log_s)
     inner, slot_in = flat & (per - 1), col & (seqs - 1)
-    pick_q = jnp.where(jnp.logical_and(owner, inner == slot_in), 1.0, 0.0)
-    pick_p = jnp.where(jnp.logical_and(owner, inner == slot_in + seqs), 1.0, 0.0)
+    pick_q = jnp.where(jnp.logical_and(owner, inner == slot_in), 1.0, 0.0).astype(BF16)
+    pick_p = jnp.where(jnp.logical_and(owner, inner == slot_in + seqs), 1.0, 0.0).astype(BF16)
     row_fold = (lax.broadcasted_iota(jnp.int32, (total_rows, total_rows), 0) & 15) >> log_p
     col_fold = (lax.broadcasted_iota(jnp.int32, (total_rows, total_rows), 1) & 15) >> log_p
     same = jnp.where(row_fold == col_fold, 1.0, 0.0)
@@ -308,8 +308,8 @@
     mine_p = jnp.where(hit_p, 1.0, 0.0).astype(BF16)
     arrive(note_pairs)
     info = notes[...].reshape(total_rows, lanes)
-    allowed = jnp.dot(pick_q.astype(BF16), info, preferred_element_type=F32)[:, :cols]
-    onehot = jnp.dot(pick_p.astype(BF16), info, preferred_element_type=F32)[:, :cols]
+    allowed = jnp.dot(pick_q, info, preferred_element_type=F32)[:, :cols]
+    onehot = jnp.dot(pick_p, info, preferred_element_type=F32)[:, :cols]
 
     for copy, origin in zip(pool_copies, behind):
         copy.wait_recv()
@@ -320,11 +320,17 @@
         relay(i)
     arrive(pool_pairs)
 
+    def three(value):
+        high = value.astype(BF16)
+        rest = value - high.astype(F32)
+        middle = rest.astype(BF16)
+        return high, middle, (rest - middle.astype(F32)).astype(BF16)
+
     x = pool[...].reshape(total_rows, fold)
     gram = lax.dot_general(x, x, NT, preferred_element_type=F32) * same
-    half = jnp.dot(pick_q, gram, preferred_element_type=F32, precision=HIGH)
-    scores = 20.0 * lax.dot_general(
-        half, pick_p, NT, preferred_element_type=F32, precision=HIGH
+    half = sum(jnp.dot(pick_q, part, preferred_element_type=F32) for part in three(gram))
+    scores = 20.0 * sum(
+        lax.dot_general(part, pick_p, NT, preferred_element_type=F32) for part in three(half)
     )
     weighted = allowed * jnp.exp(scores)
     total = jnp.sum(weighted, axis=1, keepdims=True)
@@ -332,8 +338,8 @@
     coeff = (weighted / total - onehot).astype(BF16)
     coeff_q = jnp.dot(mine_q, coeff, preferred_element_type=F32).astype(BF16)
     coeff_p = lax.dot_general(mine_p, coeff, NT, preferred_element_type=F32).astype(BF16)
-    mix = jnp.dot(coeff_q, pick_p.astype(BF16), preferred_element_type=F32)
-    mix = mix + jnp.dot(coeff_p, pick_q.astype(BF16), preferred_element_type=F32)
+    mix = jnp.dot(coeff_q, pick_p, preferred_element_type=F32)
+    mix = mix + jnp.dot(coeff_p, pick_q, preferred_element_type=F32)
     mix = (mix * same[:16, :]).astype(BF16)
     d_fold = 20.0 * jnp.dot(mix, x, preferred_element_type=F32)
     d_embed = jnp.concatenate([d_fold[i * per : (i + 1) * per, :] for i in range(folds)], axis=1)
@@ -353,20 +359,20 @@
             rows = slice(s * length, (s + 1) * length)
             inv, slope = invs[rows, 0:1], slopes[rows, 0:1]
             d_rows = inv * g_rows[s : s + 1, at] - hid[rows, at] * slope
-            for j in range(2):
-                pair = [d_rows[:, j * bw : (j + 1) * bw], d_rows[:, (2 + j) * bw : (3 + j) * bw]]
-                dhs[j, block, rows, :] = jnp.concatenate(pair, axis=1).astype(BF16)
+            for j in range(4):
+                dhs[j % 2, block, j // 2, rows, :] = d_rows[:, j * bw : (j + 1) * bw].astype(BF16)
 
     masks = list(range(nz - 1, -1, -1))
     peers = [(dc, k) for dc in range(2) for k in range(nf) if (dc, k) != (0, 0)]
     dh_copies = {}
-
-    def share(mask):
-        block = flip(z, mask)
+    halves = [(mask, away) for mask in masks for away in (1, 0)]
+
+    def share(mask, away):
+        block, side = flip(z, mask), flip(y, away)
         for dc, k in peers:
-            dh_copies[mask, dc, k] = send(
-                dhs.at[flip(core, dc), block],
-                dh_all.at[core, f, block],
+            dh_copies[mask, away, dc, k] = send(
+                dhs.at[flip(core, dc), block, side],
+                dh_all.at[core, f, block, side],
                 flip(d, dc),
                 other(k),
             )
@@ -374,7 +380,7 @@
     for place, mask in enumerate(masks):
         differentiate(flip(z, mask))
         if place < 2:
-            share(mask)
+            share(*halves[place])
     for i in range(5, 8):
         relay(i)
     col_id = lax.broadcasted_iota(jnp.int32, (cols, 1), 0)
@@ -385,28 +391,33 @@
     row_tile = min(256, depth)
     y_copies, z_copies = {}, {}
 
-    def reduce_block(place, mask):
-        block = flip(z, mask)
+    def reduce_half(place):
+        mask, away = halves[place]
+        block, side = flip(z, mask), flip(y, away)
         for dc, k in peers:
-            dh_copies[mask, dc, k].wait_recv()
-        if place + 2 < nz:
-            share(masks[place + 2])
+            dh_copies[mask, away, dc, k].wait_recv()
+        if place + 2 < len(halves):
+            share(*halves[place + 2])
 
         def step(n, carry):
             at = pl.ds(pl.multiple_of(n * row_tile, row_tile), row_tile)
-            total = jnp.dot(ctx_all[core, f, at, :], dhs[core, block], preferred_element_type=F32)
+            total = jnp.dot(
+                ctx_all[core, f, at, :], dhs[core, block, side], preferred_element_type=F32
+            )
             for dc, k in peers:
                 a, b = flip(core, dc), source(k)
                 total += jnp.dot(
-                    ctx_all[a, b, at, :], dh_all[a, b, block], preferred_element_type=F32
+                    ctx_all[a, b, at, :], dh_all[a, b, block, side], preferred_element_type=F32
                 )
-            low, high = total[:, :bw], total[:, bw:]
-            y_send[mask, at, :] = jnp.where(y == 0, high, low).astype(BF16)
-            kept[mask, at, :] = jnp.where(y == 0, low, high)
+            if away:
+                y_send[mask, at, :] = total.astype(BF16)
+            else:
+                kept[mask, at, :] = total
             return carry
 
         lax.fori_loop(0, depth // row_tile, step, 0)
-        y_copies[mask] = send(y_send.at[mask], y_recv.at[mask], flip(d, 2), f)
+        if away:
+            y_copies[mask] = send(y_send.at[mask], y_recv.at[mask], flip(d, 2), f)
 
     def forward_block(mask):
         y_copies[mask].wait_recv()
@@ -423,9 +434,10 @@
             grad_ref[...] = summed
 
     for place, mask in enumerate(masks):
-        reduce_block(place, mask)
+        reduce_half(2 * place)
         if place:
             forward_block(masks[place - 1])
+        reduce_half(2 * place + 1)
     forward_block(0)
     for copy in started:
         copy.wait_send()
@@ -467,8 +479,8 @@
             pltpu.VMEM((nd, 16, lanes), BF16),
             pltpu.VMEM((16, fold), BF16),
             pltpu.VMEM((nd, 16, fold), BF16),
-            pltpu.VMEM((2, nz, tokens, 2 * bw), BF16),
-            pltpu.VMEM((2, nf, nz, tokens, 2 * bw), BF16),
+            pltpu.VMEM((2, nz, 2, tokens, bw), BF16),
+            pltpu.VMEM((2, nf, nz, 2, tokens, bw), BF16),
             pltpu.VMEM((nz, depth, bw), BF16),
             pltpu.VMEM((nz, depth, bw), BF16),
             pltpu.VMEM((nz, depth, bw), F32),

time: 84.6 us -> 82.6 us (0.976)
  Pallas kernels: 80.8 us -> 78.8 us
    pallas_call x1, Pallas kernels: 80.8 us -> 78.8 us  [body(): pl.pallas_call(functools.partial(kernel, nd, nf, seqs), out_shape=(jax.Sh...]
where the time goes in v5:
time: 82.6 us; the launch traced here: 82.4 us
  Pallas kernels  78.8 us (95%)
  local copies, waits for them, and re-layouts  2.97 us (4%)
    pallas_call x1, Pallas kernels, body(): pl.pallas_call(functools.partial(kernel, nd, nf, seqs), out_shape=(jax.Sh...  78.8 us
    unnamed x2, local copies, waits for them, and re-layouts  2.97 us

profile of v5, /device:TPU:0, one launch (start us, length us, event | category | flops | bytes accessed | tf_op | source)
XLA Modules:
  0.0 82.4 jit_solution(9014442199576030872)
XLA Ops:
  0.6 78.8 %shard_map.77 = (f32[2]{0:T(128)}, f32[1024,128]{1,0:T(8,128)}) custom-call(bf16[256,2048]{1,0:T(8,128)(2,1)} %context_hbm.1, bf16[256,2048]{1,0:T(8,128)(2,1)} %residual_hbm.1, bf16[1024,2048]{1,0:T(8,128)(2,1)} %weight_hbm.1, bf16[2048]{0:T(1024)(128)(2,1)} %gain_hbm.1, s32[1,16]{1,0:T(1,128)} %pattern_hbm.1, s32[2]{0:T(128)} %positive_ref.1), custom_call_target="tpu_custom_call" | custom-call | flops 8589934592 | bytes 16777216 | tf_op jit(solution)/shard_map/pallas_call | solution.py:458
  79.4 1.1 %copy.10 = f32[2]{0:T(128)} copy(f32[2]{0:T(128)} %get-tuple-element.4) | data formatting | bytes 16
  80.5 1.9 %copy.11 = f32[1024,128]{1,0:T(8,128)} copy(f32[1024,128]{1,0:T(8,128)} %get-tuple-element.5) | data formatting | bytes 1048576

commit v6 on v5

--- a/solution.py
+++ b/solution.py
@@ -26,7 +26,7 @@
 def count_copies(nd, nf):
     nz = nd // 4
     groups = nd // 2
-    weights = (nf - 1) * (4 + 2 + 5 + 5 + 16)
+    weights = (nf - 1) * 8 * 8
     return weights + 16 * (nf - 1) + 1 + 4 * groups + (2 * nf - 1) * 2 * nz + nz + nz - 1
 
 
@@ -79,7 +79,7 @@
     z = lax.div(d, 4)
     spot = lax.rem(d, 8)
     length = tokens // (2 * seqs)
-    parts = 4
+    parts = 8
     rows_in = depth // 8
     wide = width // parts
     other = lambda k: lax.rem(f + k, nf)
@@ -163,8 +163,8 @@
         meta = jnp.where(hit, 1.0, meta)
     note[...] = meta.astype(BF16)
     notes[d] = note[...]
-    near = [lax.rem(d + 2 * s, nd) for s in range(1, nd // 2)]
-    behind = [lax.rem(d + nd - 2 * s, nd) for s in range(1, nd // 2)]
+    near = [lax.rem(d + 2 * s, nd) for s in range(nd // 2 - 1, 0, -1)]
+    behind = [lax.rem(d + nd - 2 * s, nd) for s in range(nd // 2 - 1, 0, -1)]
     note_copies = [send(note, notes.at[d], there, f) for there in near]
     note_pairs = [send(note, notes.at[d], sibling, f)]
 
@@ -188,19 +188,7 @@
 
         lax.fori_loop(start // tile, (start + count) // tile, step, 0)
 
-    arrive(direct[0])
-    to_y, to_z, to_core, straight = {}, {}, {h: [] for h in range(parts)}, {}
-
-    def spread_out(h):
-        to_y[h] = pass_on(spot, h, 2)
-        to_z[h] = pass_on(spot, h, 4)
-        to_core[h] += pass_on(spot, h, 1)
-
-    def finish(h):
-        arrive(to_core[h])
-        for k in others:
-            project(source(k), False, h * wide, wide)
-
+    to_y, to_z, to_core, to_far = {}, {}, {h: [] for h in range(parts)}, {}
     chunks = 8
     ctx_copies = {}
 
@@ -218,54 +206,54 @@
             ref = ctx_all.at[core, source(k), chunk(i)]
             sibling_ctx.append(send(ref, ref, sibling, f))
 
-    spread_out(0)
-    direct[2], straight[2] = fetch(spot, 2), fetch(far, 2)
-    project(f, True, 0, width)
-    arrive(direct[1])
-    spread_out(1)
-    direct[3], straight[3] = fetch(spot, 3), fetch(far, 3)
-    arrive(to_z[0])
-    across_y = pass_on(near_z, 0, 2)
-    to_core[0] += pass_on(near_z, 0, 1)
-    arrive(to_y[0])
-    to_core[0] += pass_on(near_y, 0, 1)
-    arrive(direct[2])
-    spread_out(2)
-    arrive(to_y[1])
-    across_z = pass_on(near_y, 1, 4)
-    to_core[1] += pass_on(near_y, 1, 1)
-    arrive(to_z[1])
-    to_core[1] += pass_on(near_z, 1, 1)
-    arrive(straight[2])
-    to_core[2] += pass_on(far, 2, 1)
-    arrive(across_y)
-    to_core[0] += pass_on(far, 0, 1)
-    arrive(direct[3])
-    spread_out(3)
-    trickle(0)
-    finish(0)
-    trickle(1)
-    arrive(across_z)
-    to_core[1] += pass_on(far, 1, 1)
-    arrive(to_y[2])
-    to_core[2] += pass_on(near_y, 2, 1)
-    arrive(to_z[2])
-    to_core[2] += pass_on(near_z, 2, 1)
-    arrive(straight[3])
-    to_core[3] += pass_on(far, 3, 1)
-    trickle(2)
-    finish(1)
-    trickle(3)
-    finish(2)
-    arrive(to_y[3])
-    to_core[3] += pass_on(near_y, 3, 1)
-    arrive(to_z[3])
-    to_core[3] += pass_on(near_z, 3, 1)
-    for copy, origin in zip(note_copies, behind):
-        copy.wait_recv()
-        note_pairs.append(send(notes.at[origin], notes.at[origin], sibling, f))
-    trickle(4)
-    finish(3)
+    by_y, by_z = range(0, parts // 4), range(parts // 4, parts // 2)
+
+    def from_x(h):
+        arrive(direct[h])
+        to_y[h] = pass_on(spot, h, 2)
+        to_z[h] = pass_on(spot, h, 4)
+        to_core[h] += pass_on(spot, h, 1)
+        if h + 2 < parts:
+            direct[h + 2] = fetch(spot, h + 2)
+            if h + 2 >= parts // 2:
+                to_far[h + 2] = fetch(far, h + 2)
+
+    def from_near(h):
+        for copies, place, turn, routed in (
+            (to_z[h], near_z, 2, by_y),
+            (to_y[h], near_y, 4, by_z),
+        ):
+            arrive(copies)
+            if h in routed:
+                to_far[h] = pass_on(place, h, turn)
+            to_core[h] += pass_on(place, h, 1)
+
+    def from_far(h):
+        arrive(to_far[h])
+        to_core[h] += pass_on(far, h, 1)
+
+    def finish(h):
+        arrive(to_core[h])
+        for k in others:
+            project(source(k), False, h * wide, wide)
+
+    for t in range(parts + 3):
+        if t < parts:
+            from_x(t)
+        if t == 0:
+            project(f, True, 0, width)
+        if 0 <= t - 1 < parts:
+            from_near(t - 1)
+        if 0 <= t - 2 < parts:
+            from_far(t - 2)
+        if t >= parts - 1:
+            trickle(t - parts + 1)
+        if t == parts:
+            for copy, origin in zip(note_copies, behind):
+                copy.wait_recv()
+                note_pairs.append(send(notes.at[origin], notes.at[origin], sibling, f))
+        if t >= 3:
+            finish(t - 3)
 
     loads[3].wait()
     gain = gain_ref[...].astype(F32).reshape(1, width)
@@ -314,9 +302,9 @@
     for copy, origin in zip(pool_copies, behind):
         copy.wait_recv()
         pool_pairs.append(send(pool.at[origin], pool.at[origin], sibling, f))
-    for i in range(5, 8):
+    for i in range(4, 8):
         trickle(i)
-    for i in range(5):
+    for i in range(4):
         relay(i)
     arrive(pool_pairs)
 
@@ -365,7 +353,10 @@
     masks = list(range(nz - 1, -1, -1))
     peers = [(dc, k) for dc in range(2) for k in range(nf) if (dc, k) != (0, 0)]
     dh_copies = {}
-    halves = [(mask, away) for mask in masks for away in (1, 0)]
+    halves = [(masks[0], 1)]
+    for ahead, mask in zip(masks[1:], masks):
+        halves += [(ahead, 1), (mask, 0)]
+    halves.append((masks[-1], 0))
 
     def share(mask, away):
         block, side = flip(z, mask), flip(y, away)
@@ -381,7 +372,7 @@
         differentiate(flip(z, mask))
         if place < 2:
             share(*halves[place])
-    for i in range(5, 8):
+    for i in range(4, 8):
         relay(i)
     col_id = lax.broadcasted_iota(jnp.int32, (cols, 1), 0)
     for s in range(seqs):
@@ -433,12 +424,10 @@
         else:
             grad_ref[...] = summed
 
-    for place, mask in enumerate(masks):
-        reduce_half(2 * place)
-        if place:
-            forward_block(masks[place - 1])
-        reduce_half(2 * place + 1)
-    forward_block(0)
+    for place, (mask, away) in enumerate(halves):
+        reduce_half(place)
+        if not away:
+            forward_block(mask)
     for copy in started:
         copy.wait_send()
 

time: 82.6 us -> 88.2 us (1.068)
  Pallas kernels: 78.8 us -> 84.4 us
    pallas_call x1, Pallas kernels: 78.8 us -> 84.4 us  [body(): pl.pallas_call(functools.partial(kernel, nd, nf, seqs), out_shape=(jax.Sh...]
where the time goes in v6:
time: 88.2 us; the launch traced here: 88 us
  Pallas kernels  84.4 us (96%)
  local copies, waits for them, and re-layouts  2.97 us (3%)
    pallas_call x1, Pallas kernels, body(): pl.pallas_call(functools.partial(kernel, nd, nf, seqs), out_shape=(jax.Sh...  84.4 us
    unnamed x2, local copies, waits for them, and re-layouts  2.97 us

profile of v6, /device:TPU:0, one launch (start us, length us, event | category | flops | bytes accessed | tf_op | source)
XLA Modules:
  0.0 88.0 jit_solution(16206717781827291185)
XLA Ops:
  0.6 84.4 %shard_map.77 = (f32[2]{0:T(128)}, f32[1024,128]{1,0:T(8,128)}) custom-call(bf16[256,2048]{1,0:T(8,128)(2,1)} %context_hbm.1, bf16[256,2048]{1,0:T(8,128)(2,1)} %residual_hbm.1, bf16[1024,2048]{1,0:T(8,128)(2,1)} %weight_hbm.1, bf16[2048]{0:T(1024)(128)(2,1)} %gain_hbm.1, s32[1,16]{1,0:T(1,128)} %pattern_hbm.1, s32[2]{0:T(128)} %positive_ref.1), custom_call_target="tpu_custom_call" | custom-call | flops 8589934592 | bytes 16777216 | tf_op jit(solution)/shard_map/pallas_call | solution.py:447
  85.0 1.1 %copy.10 = f32[2]{0:T(128)} copy(f32[2]{0:T(128)} %get-tuple-element.4) | data formatting | bytes 16
  86.1 1.9 %copy.11 = f32[1024,128]{1,0:T(8,128)} copy(f32[1024,128]{1,0:T(8,128)} %get-tuple-element.5) | data formatting | bytes 1048576

commit v7 on v5

--- a/solution.py
+++ b/solution.py
@@ -201,7 +201,7 @@
         for k in others:
             project(source(k), False, h * wide, wide)
 
-    chunks = 8
+    chunks = 1
     ctx_copies = {}
 
     def chunk(i):
@@ -244,7 +244,6 @@
     spread_out(3)
     trickle(0)
     finish(0)
-    trickle(1)
     arrive(across_z)
     to_core[1] += pass_on(far, 1, 1)
     arrive(to_y[2])
@@ -253,9 +252,7 @@
     to_core[2] += pass_on(near_z, 2, 1)
     arrive(straight[3])
     to_core[3] += pass_on(far, 3, 1)
-    trickle(2)
     finish(1)
-    trickle(3)
     finish(2)
     arrive(to_y[3])
     to_core[3] += pass_on(near_y, 3, 1)
@@ -264,7 +261,6 @@
     for copy, origin in zip(note_copies, behind):
         copy.wait_recv()
         note_pairs.append(send(notes.at[origin], notes.at[origin], sibling, f))
-    trickle(4)
     finish(3)
 
     loads[3].wait()
@@ -314,10 +310,7 @@
     for copy, origin in zip(pool_copies, behind):
         copy.wait_recv()
         pool_pairs.append(send(pool.at[origin], pool.at[origin], sibling, f))
-    for i in range(5, 8):
-        trickle(i)
-    for i in range(5):
-        relay(i)
+    relay(0)
     arrive(pool_pairs)
 
     def three(value):
@@ -365,7 +358,10 @@
     masks = list(range(nz - 1, -1, -1))
     peers = [(dc, k) for dc in range(2) for k in range(nf) if (dc, k) != (0, 0)]
     dh_copies = {}
-    halves = [(mask, away) for mask in masks for away in (1, 0)]
+    halves = [(masks[0], 1)]
+    for ahead, mask in zip(masks[1:], masks):
+        halves += [(ahead, 1), (mask, 0)]
+    halves.append((masks[-1], 0))
 
     def share(mask, away):
         block, side = flip(z, mask), flip(y, away)
@@ -381,11 +377,12 @@
         differentiate(flip(z, mask))
         if place < 2:
             share(*halves[place])
-    for i in range(5, 8):
-        relay(i)
     col_id = lax.broadcasted_iota(jnp.int32, (cols, 1), 0)
     for s in range(seqs):
         loss_ref[s] = jnp.sum(jnp.where(col_id == d * seqs + s, losses, 0.0))
+    first_shared = len(started) - 2 * len(peers)
+    for copy in started[:first_shared]:
+        copy.wait_send()
     arrive(sibling_ctx)
 
     row_tile = min(256, depth)
@@ -433,13 +430,11 @@
         else:
             grad_ref[...] = summed
 
-    for place, mask in enumerate(masks):
-        reduce_half(2 * place)
-        if place:
-            forward_block(masks[place - 1])
-        reduce_half(2 * place + 1)
-    forward_block(0)
-    for copy in started:
+    for place, (mask, away) in enumerate(halves):
+        reduce_half(place)
+        if not away:
+            forward_block(mask)
+    for copy in started[first_shared:]:
         copy.wait_send()
 
 

time: 82.6 us -> 81.1 us (0.982)
  Pallas kernels: 78.8 us -> 77.3 us
    pallas_call x1, Pallas kernels: 78.8 us -> 77.3 us  [body(): pl.pallas_call(functools.partial(kernel, nd, nf, seqs), out_shape=(jax.Sh...]
where the time goes in v7:
time: 81.1 us; the launch traced here: 80.9 us
  Pallas kernels  77.3 us (95%)
  local copies, waits for them, and re-layouts  2.97 us (4%)
    pallas_call x1, Pallas kernels, body(): pl.pallas_call(functools.partial(kernel, nd, nf, seqs), out_shape=(jax.Sh...  77.3 us
    unnamed x2, local copies, waits for them, and re-layouts  2.97 us

profile of v7, /device:TPU:0, one launch (start us, length us, event | category | flops | bytes accessed | tf_op | source)
XLA Modules:
  0.0 80.9 jit_solution(4877245676944117065)
XLA Ops:
  0.6 77.3 %shard_map.77 = (f32[2]{0:T(128)}, f32[1024,128]{1,0:T(8,128)}) custom-call(bf16[256,2048]{1,0:T(8,128)(2,1)} %context_hbm.1, bf16[256,2048]{1,0:T(8,128)(2,1)} %residual_hbm.1, bf16[1024,2048]{1,0:T(8,128)(2,1)} %weight_hbm.1, bf16[2048]{0:T(1024)(128)(2,1)} %gain_hbm.1, s32[1,16]{1,0:T(1,128)} %pattern_hbm.1, s32[2]{0:T(128)} %positive_ref.1), custom_call_target="tpu_custom_call" | custom-call | flops 8589934592 | bytes 16777216 | tf_op jit(solution)/shard_map/pallas_call | solution.py:453
  77.9 1.1 %copy.10 = f32[2]{0:T(128)} copy(f32[2]{0:T(128)} %get-tuple-element.4) | data formatting | bytes 16
  79.0 1.9 %copy.11 = f32[1024,128]{1,0:T(8,128)} copy(f32[1024,128]{1,0:T(8,128)} %get-tuple-element.5) | data formatting | bytes 1048576

commit v8 on v7

--- a/solution.py
+++ b/solution.py
@@ -126,7 +126,8 @@
     near_y, near_z, far = flip(spot, 2), flip(spot, 4), flip(spot, 6)
 
     def piece(place, h):
-        return (pl.ds(pl.multiple_of(place * rows_in, rows_in), rows_in), slice(h * wide, (h + 1) * wide))
+        row = (lax.rem(place, 2) * 4 + lax.div(place, 2)) * rows_in
+        return (pl.ds(pl.multiple_of(row, rows_in), rows_in), slice(h * wide, (h + 1) * wide))
 
     def fetch(place, h):
         at = piece(place, h)
@@ -146,6 +147,9 @@
 
     direct = {0: fetch(spot, 0)}
 
+    groups = nd // 2
+    slot_of_d = core * groups + lax.div(d, 2)
+    core_slots = pl.ds(core * groups, groups)
     loads[4].wait()
     lanes = note.shape[1]
     lane_id = lax.broadcasted_iota(jnp.int32, (16, lanes), 1)
@@ -162,11 +166,9 @@
         hit = jnp.logical_and(row_id == seqs + s, lane_id == positive_ref[s] + d * seqs)
         meta = jnp.where(hit, 1.0, meta)
     note[...] = meta.astype(BF16)
-    notes[d] = note[...]
+    notes[slot_of_d] = note[...]
     near = [lax.rem(d + 2 * s, nd) for s in range(1, nd // 2)]
-    behind = [lax.rem(d + nd - 2 * s, nd) for s in range(1, nd // 2)]
-    note_copies = [send(note, notes.at[d], there, f) for there in near]
-    note_pairs = [send(note, notes.at[d], sibling, f)]
+    note_copies = [send(note, notes.at[slot_of_d], there, f) for there in near]
 
     loads[0].wait()
     for part in range(nf):
@@ -194,7 +196,12 @@
     def spread_out(h):
         to_y[h] = pass_on(spot, h, 2)
         to_z[h] = pass_on(spot, h, 4)
-        to_core[h] += pass_on(spot, h, 1)
+
+    def to_sibling(h):
+        rows = pl.ds(pl.multiple_of(core * 4 * rows_in, rows_in), 4 * rows_in)
+        for k in others:
+            ref = wg.at[source(k), rows, slice(h * wide, (h + 1) * wide)]
+            to_core[h].append(send(ref, ref, sibling, f))
 
     def finish(h):
         arrive(to_core[h])
@@ -226,41 +233,32 @@
     direct[3], straight[3] = fetch(spot, 3), fetch(far, 3)
     arrive(to_z[0])
     across_y = pass_on(near_z, 0, 2)
-    to_core[0] += pass_on(near_z, 0, 1)
-    arrive(to_y[0])
-    to_core[0] += pass_on(near_y, 0, 1)
     arrive(direct[2])
     spread_out(2)
+    arrive(to_y[0])
     arrive(to_y[1])
     across_z = pass_on(near_y, 1, 4)
-    to_core[1] += pass_on(near_y, 1, 1)
-    arrive(to_z[1])
-    to_core[1] += pass_on(near_z, 1, 1)
-    arrive(straight[2])
-    to_core[2] += pass_on(far, 2, 1)
     arrive(across_y)
-    to_core[0] += pass_on(far, 0, 1)
+    to_sibling(0)
     arrive(direct[3])
     spread_out(3)
     trickle(0)
+    arrive(to_z[1])
+    arrive(across_z)
+    to_sibling(1)
     finish(0)
-    arrive(across_z)
-    to_core[1] += pass_on(far, 1, 1)
+    arrive(straight[2])
     arrive(to_y[2])
-    to_core[2] += pass_on(near_y, 2, 1)
     arrive(to_z[2])
-    to_core[2] += pass_on(near_z, 2, 1)
+    to_sibling(2)
+    finish(1)
     arrive(straight[3])
-    to_core[3] += pass_on(far, 3, 1)
-    finish(1)
+    arrive(to_y[3])
+    arrive(to_z[3])
+    to_sibling(3)
     finish(2)
-    arrive(to_y[3])
-    to_core[3] += pass_on(near_y, 3, 1)
-    arrive(to_z[3])
-    to_core[3] += pass_on(near_z, 3, 1)
-    for copy, origin in zip(note_copies, behind):
-        copy.wait_recv()
-        note_pairs.append(send(notes.at[origin], notes.at[origin], sibling, f))
+    arrive(note_copies)
+    note_pairs = [send(notes.at[core_slots], notes.at[core_slots], sibling, f)]
     finish(3)
 
     loads[3].wait()
@@ -280,16 +278,17 @@
     fold = width // folds
     folded = jnp.concatenate([unit[:, i * fold : (i + 1) * fold] for i in range(folds)], axis=0)
     msg[...] = folded.astype(BF16)
-    pool_copies = [send(msg, pool.at[d], there, f) for there in near]
-    pool_pairs = [send(msg, pool.at[d], sibling, f)]
-    pool[d] = msg[...]
+    pool_copies = [send(msg, pool.at[slot_of_d], there, f) for there in near]
+    pool[slot_of_d] = msg[...]
 
     cols = nd * seqs
     total_rows = nd * 16
     log_p = per.bit_length() - 1
     flat = lax.broadcasted_iota(jnp.int32, (cols, total_rows), 1)
     col = lax.broadcasted_iota(jnp.int32, (cols, total_rows), 0)
-    owner = (flat >> 4) == (col >> log_s)
+    log_g = groups.bit_length() - 1
+    device = (((flat >> 4) & (groups - 1)) << 1) + (flat >> (4 + log_g))
+    owner = device == (col >> log_s)
     inner, slot_in = flat & (per - 1), col & (seqs - 1)
     pick_q = jnp.where(jnp.logical_and(owner, inner == slot_in), 1.0, 0.0).astype(BF16)
     pick_p = jnp.where(jnp.logical_and(owner, inner == slot_in + seqs), 1.0, 0.0).astype(BF16)
@@ -307,9 +306,8 @@
     allowed = jnp.dot(pick_q, info, preferred_element_type=F32)[:, :cols]
     onehot = jnp.dot(pick_p, info, preferred_element_type=F32)[:, :cols]
 
-    for copy, origin in zip(pool_copies, behind):
-        copy.wait_recv()
-        pool_pairs.append(send(pool.at[origin], pool.at[origin], sibling, f))
+    arrive(pool_copies)
+    pool_pairs = [send(pool.at[core_slots], pool.at[core_slots], sibling, f)]
     relay(0)
     arrive(pool_pairs)
 

time: 81.1 us -> 80.5 us (level)
  no operation moved by 1% of the time
where the time goes in v8:
time: 80.5 us; the launch traced here: 80.3 us
  Pallas kernels  76.7 us (95%)
  local copies, waits for them, and re-layouts  2.97 us (4%)
    pallas_call x1, Pallas kernels, body(): pl.pallas_call(functools.partial(kernel, nd, nf, seqs), out_shape=(jax.Sh...  76.7 us
    unnamed x2, local copies, waits for them, and re-layouts  2.97 us

profile of v8, /device:TPU:0, one launch (start us, length us, event | category | flops | bytes accessed | tf_op | source)
XLA Modules:
  0.0 80.3 jit_solution(12106875727346898436)
XLA Ops:
  0.6 76.7 %shard_map.77 = (f32[2]{0:T(128)}, f32[1024,128]{1,0:T(8,128)}) custom-call(bf16[256,2048]{1,0:T(8,128)(2,1)} %context_hbm.1, bf16[256,2048]{1,0:T(8,128)(2,1)} %residual_hbm.1, bf16[1024,2048]{1,0:T(8,128)(2,1)} %weight_hbm.1, bf16[2048]{0:T(1024)(128)(2,1)} %gain_hbm.1, s32[1,16]{1,0:T(1,128)} %pattern_hbm.1, s32[2]{0:T(128)} %positive_ref.1), custom_call_target="tpu_custom_call" | custom-call | flops 8589934592 | bytes 16777216 | tf_op jit(solution)/shard_map/pallas_call | solution.py:451
  77.4 1.1 %copy.10 = f32[2]{0:T(128)} copy(f32[2]{0:T(128)} %get-tuple-element.4) | data formatting | bytes 16
  78.5 1.9 %copy.11 = f32[1024,128]{1,0:T(8,128)} copy(f32[1024,128]{1,0:T(8,128)} %get-tuple-element.5) | data formatting | bytes 1048576

commit v9 on v8

--- a/solution.py
+++ b/solution.py
@@ -375,10 +375,12 @@
         differentiate(flip(z, mask))
         if place < 2:
             share(*halves[place])
+        if place == 1:
+            share(*halves[2])
     col_id = lax.broadcasted_iota(jnp.int32, (cols, 1), 0)
     for s in range(seqs):
         loss_ref[s] = jnp.sum(jnp.where(col_id == d * seqs + s, losses, 0.0))
-    first_shared = len(started) - 2 * len(peers)
+    first_shared = len(started) - 3 * len(peers)
     for copy in started[:first_shared]:
         copy.wait_send()
     arrive(sibling_ctx)
@@ -391,8 +393,8 @@
         block, side = flip(z, mask), flip(y, away)
         for dc, k in peers:
             dh_copies[mask, away, dc, k].wait_recv()
-        if place + 2 < len(halves):
-            share(*halves[place + 2])
+        if place + 3 < len(halves):
+            share(*halves[place + 3])
 
         def step(n, carry):
             at = pl.ds(pl.multiple_of(n * row_tile, row_tile), row_tile)

time: 80.5 us -> 80.5 us (level)
  no operation moved by 1% of the time
where the time goes in v9:
time: 80.5 us; the launch traced here: 80.3 us
  Pallas kernels  76.7 us (95%)
  local copies, waits for them, and re-layouts  2.97 us (4%)
    pallas_call x1, Pallas kernels, body(): pl.pallas_call(functools.partial(kernel, nd, nf, seqs), out_shape=(jax.Sh...  76.7 us
    unnamed x2, local copies, waits for them, and re-layouts  2.97 us

profile of v9, /device:TPU:0, one launch (start us, length us, event | category | flops | bytes accessed | tf_op | source)
XLA Modules:
  0.0 80.3 jit_solution(11266803410376236328)
XLA Ops:
  0.6 76.7 %shard_map.77 = (f32[2]{0:T(128)}, f32[1024,128]{1,0:T(8,128)}) custom-call(bf16[256,2048]{1,0:T(8,128)(2,1)} %context_hbm.1, bf16[256,2048]{1,0:T(8,128)(2,1)} %residual_hbm.1, bf16[1024,2048]{1,0:T(8,128)(2,1)} %weight_hbm.1, bf16[2048]{0:T(1024)(128)(2,1)} %gain_hbm.1, s32[1,16]{1,0:T(1,128)} %pattern_hbm.1, s32[2]{0:T(128)} %positive_ref.1), custom_call_target="tpu_custom_call" | custom-call | flops 8589934592 | bytes 16777216 | tf_op jit(solution)/shard_map/pallas_call | solution.py:453
  77.4 1.1 %copy.10 = f32[2]{0:T(128)} copy(f32[2]{0:T(128)} %get-tuple-element.4) | data formatting | bytes 16
  78.5 1.9 %copy.11 = f32[1024,128]{1,0:T(8,128)} copy(f32[1024,128]{1,0:T(8,128)} %get-tuple-element.5) | data formatting | bytes 1048576
